TPU v7x, 128 devices: a whole 4x4x4 slice. The times are simulated.
128 devices in a mesh: src: 8 (over x, core), tgt: 16 (over z, y).
Axes of the slice: x: 4, y: 4, z: 4, core: 2. Of those that a mesh axis runs over, the one named last changes fastest.
Arguments:
- source_fields: float32 [7, 524288], P(None, ('src', 'tgt'))
- slot_source: int32 [8388608], P(('src', 'tgt')), may hold values from 0 to 4095
- slot_weight: float32 [8388608], P(('src', 'tgt')), may hold values from 0.05 to 1
- slot_target: int32 [8388608], P(('src', 'tgt')), may hold values from -1 to 8191, as said below
- cell_mass: float32 [32, 256, 128], P('src', 'tgt'), may hold values from 0.5 to 2
- send_order: int32 [128, 8192], P(('src', 'tgt')), may hold values from 0 to 8191, each once within a row
- place_order: int32 [128, 8192], P(('src', 'tgt')), may hold values from 0 to 8191, each once within a row
Outputs:
- projected: float32 [7, 32, 256, 128], P(None, 'src', 'tgt')
- moduli: float32 [3, 1048576], P(None, ('src', 'tgt'))
Inputs may be any that keep to these rules, and one draw needn't show every extreme that they name: `slot_target`: within each sending partition's block of 512 slots at an owner, the live slots come first and there are 128 or more of them; some owner has all 512 slots live from every sender.
All inputs are finite; a program needn't handle non-finite values.
Results may differ from a plain program's by a relative error of at most 0.00007.
Values sent between devices are 32-bit elements; how exact they have to be, the bound alone decides.
A program may use at most 64 MiB of HBM per device.

v0:
```python
import math

import jax
import jax.numpy as jnp
from jax import lax
from jax.sharding import PartitionSpec as P

ITERS = 4


def padded_2(x, sides, width):
    for axis, dim in sides:
        count, length = (lax.axis_size(axis), x.shape[dim])
        up = [(i, (i + 1) % count) for i in range(count - 1)]
        down = [(j, i) for i, j in up]
        last = lax.slice_in_dim(x, length - width, length, axis=dim)
        first = lax.slice_in_dim(x, 0, width, axis=dim)
        before = lax.ppermute(last, axis, up)
        after = lax.ppermute(first, axis, down)
        x = jnp.concatenate([before, x, after], axis=dim)
    return x


def cell_moduli(vals):
    phi = vals[0]
    mean = (vals[1] + vals[2] + vals[3]) / 3.0
    q2 = 1.5 * (
        (vals[1] - mean) ** 2
        + (vals[2] - mean) ** 2
        + (vals[3] - mean) ** 2
        + 2.0 * (vals[4] ** 2 + vals[5] ** 2 + vals[6] ** 2)
    )
    bulk = 1.6 * jnp.exp(-3.0 * phi) * (1.0 + 0.25 * jnp.tanh(mean))
    shear = 0.9 * jnp.exp(-2.0 * phi) / (1.0 + q2 / 0.5)
    soften = shear * q2 / (0.5 + q2)
    return jnp.stack([bulk, shear, soften])


def lookup_columns(table, index):
    rows, width = table.shape
    groups = width // 32
    folded = table.reshape(rows, groups, 32).transpose(0, 2, 1).reshape(rows * 32, groups)
    count = index.shape[0]
    block = math.gcd(count, 4096)
    group_ids = jnp.arange(groups, dtype=jnp.int32)
    lane_ids = jnp.arange(32, dtype=jnp.int32)

    def one_block(piece):
        onehot = (piece[None, :] // 32 == group_ids[:, None]).astype(jnp.float32)
        picked = jnp.dot(
            folded, onehot, precision=lax.Precision.HIGHEST, preferred_element_type=jnp.float32
        ).reshape(rows, 32, piece.shape[0])
        lanes = (piece[None, :] % 32 == lane_ids[:, None]).astype(jnp.float32)
        return jnp.sum(picked * lanes[None], axis=1)

    pieces = lax.map(one_block, index.reshape(count // block, block))
    return pieces.transpose(1, 0, 2).reshape(rows, count)


def spread_columns(values, index, width):
    rows, count = values.shape
    groups = width // 32
    block = math.gcd(count, 4096)
    blocks = count // block
    group_ids = jnp.arange(groups, dtype=jnp.int32)
    lane_ids = jnp.arange(32, dtype=jnp.int32)
    value_blocks = values.reshape(rows, blocks, block).transpose(1, 0, 2)
    index_blocks = index.reshape(blocks, block)

    def add_block(total, inputs):
        vals, piece = inputs
        onehot = (piece[:, None] // 32 == group_ids[None, :]).astype(jnp.float32)
        lanes = (piece[:, None] % 32 == lane_ids[None, :]).astype(jnp.float32)
        spread = (vals.T[:, :, None] * lanes[:, None, :]).reshape(block, rows * 32)
        added = lax.dot_general(
            onehot,
            spread,
            (((0,), (0,)), ((), ())),
            precision=lax.Precision.HIGHEST,
            preferred_element_type=jnp.float32,
        )
        return (total + added, None)

    start = jnp.zeros((groups, rows * 32), jnp.float32)
    total, _ = lax.scan(add_block, start, (value_blocks, index_blocks))
    return total.reshape(groups, rows, 32).transpose(1, 0, 2).reshape(rows, width)


def mass_apply(field, root):
    w = root[None] * field
    padded = padded_2(w, (("src", 1), ("tgt", 2)), 1)
    deep = jnp.pad(w, ((0, 0), (0, 0), (0, 0), (1, 1)))
    nb = padded[:, 2:, 1:-1] + padded[:, :-2, 1:-1]
    nb = nb + padded[:, 1:-1, 2:] + padded[:, 1:-1, :-2]
    nb = nb + deep[:, :, :, 2:] + deep[:, :, :, :-2]
    return root[None] * (w + 0.125 * nb)


def on_device(
    source_fields, slot_source, slot_weight, slot_target, cell_mass, send_order, place_order
):
    n_src = lax.axis_size("src")
    n_tgt = lax.axis_size("tgt")
    owners = n_src * n_tgt
    per_owner = slot_source.shape[0] // owners
    hx_cells, hy_cells, hz_cells = cell_mass.shape
    cells = hx_cells * hy_cells * hz_cells
    quota = cells // owners
    values = slot_weight[None, :] * lookup_columns(source_fields, slot_source)
    values = values.reshape(7, owners, per_owner)
    arrived = lax.all_to_all(values, ("src", "tgt"), split_axis=1, concat_axis=1, tiled=True)
    arrived = arrived.reshape(7, owners * per_owner)
    rhs = spread_columns(arrived, slot_target, cells)
    rhs = rhs.reshape(7, hx_cells, hy_cells, hz_cells)
    root = jnp.sqrt(cell_mass)
    theta = 1.0
    delta = 0.75
    sigma = theta / delta
    rho = 1.0 / sigma
    solution = jnp.zeros_like(rhs)
    resid = rhs
    direction = resid / (theta * cell_mass[None])
    for sweep in range(ITERS):
        image = mass_apply(direction, root)
        solution = solution + direction
        resid = resid - image
        rho_new = 1.0 / (2.0 * sigma - rho)
        direction = rho_new * rho * direction + 2.0 * rho_new / delta * resid / cell_mass[None]
        rho = rho_new
    projected = solution + direction
    flat = projected.reshape(7, cells)
    payload = cell_moduli(flat)
    rows = payload.shape[0]
    outgoing = lookup_columns(payload, send_order[0])
    incoming = lax.all_to_all(
        outgoing.reshape(rows, owners, quota),
        ("src", "tgt"),
        split_axis=1,
        concat_axis=1,
        tiled=True,
    )
    placed = lookup_columns(incoming.reshape(rows, cells), place_order[0])
    return (projected, placed)


def solution(mesh):
    placed = (
        P(None, ("src", "tgt")),
        P(("src", "tgt")),
        P(("src", "tgt")),
        P(("src", "tgt")),
        P("src", "tgt", None),
        P(("src", "tgt"), None),
        P(("src", "tgt"), None),
    )
    return jax.shard_map(
        on_device,
        mesh=mesh,
        in_specs=placed,
        out_specs=(P(None, "src", "tgt", None), P(None, ("src", "tgt"))),
        check_vma=False,
    )
```

profile of v0, /device:TPU:1, one launch (start us, length us, event | category | flops | bytes accessed | tf_op | source)
XLA Modules:
  0.0 307.5 jit_solution(887429715641421079)
XLA Ops:
  2.9 39.0 %while.52 = (s32[]{:T(128)}, f32[16,7,4096]{2,1,0:T(8,128)S(1)}, s32[16,4096]{1,0:T(8,128)S(1)}, f32[224,128]{1,0:T(8,128)S(1)}, s32[]{:T(128)}) while((s32[]{:T(128)}, f32[16,7,4096]{2,1,0:T(8,128)S(1)}, s32[16,4096]{1,0:T(8,128)S(1)}, f32[224,128]{1,0:T(8,128)S(1)}, s32[]{:T(128)}) %tuple.153), condition=%wide.region_2.3_spmd.clone, body=%wide.region_0.2_spmd.clone.sunk | while | flops 1411973120 | bytes 9011273 | solution.py:56
  48.7 11.5 %all-to-all-start = ((f32[7,128,512]{2,0,1:T(8,128)}), f32[7,128,512]{2,0,1:T(8,128)S(1)}, u32[]{:S(2)}, u32[]{:S(2)}) async-start(f32[7,128,512]{2,0,1:T(8,128)} %copy.42), calls=%async_computation | async-start | bytes 4194304 | tf_op jit(solution)/shard_map/all_to_all | solution.py:111
  60.3 29.1 %all-to-all-done = f32[7,128,512]{2,0,1:T(8,128)S(1)} async-done(((f32[7,128,512]{2,0,1:T(8,128)}), f32[7,128,512]{2,0,1:T(8,128)S(1)}, u32[]{:S(2)}, u32[]{:S(2)}) %all-to-all-start) | async-done | bytes 1835040 | tf_op jit(solution)/shard_map/all_to_all | solution.py:111
  93.4 112.1 %while.55 = (s32[]{:T(128)}, f32[256,224]{0,1:T(8,128)S(1)}, s32[16,4096]{1,0:T(8,128)S(1)}, f32[16,7,4096]{2,0,1:T(8,128)S(1)}, s32[]{:T(128)}, /*index=5*/s32[]{:T(128)}) while((s32[]{:T(128)}, f32[256,224]{0,1:T(8,128)S(1)}, s32[16,4096]{1,0:T(8,128)S(1)}, f32[16,7,4096]{2,0,1:T(8,128)S(1)}, s32[]{:T(128)}, ...), condition=%wide.region_4.5_spmd.clone, body=%wide.region_3.4_spmd.clone.sunk | while | flops 2820993024 | bytes 9535575 | solution.py:85
  95.8 4.5 %fusion.109 = f32[256,224]{0,1:T(8,128)S(1)} fusion(f32[4096,224]{0,1:T(8,128)} %bitcast.101, s32[4096]{0:T(1024)S(1)} %get-tuple-element.581, f32[256,224]{0,1:T(8,128)S(1)} %get-tuple-element.604, pred[]{:T(512)S(6)} %compare.42), kind=kOutput, calls=%fused_computation.48.clone.1 | convolution fusion | flops 2819735552 | bytes 4145153 | tf_op jit(solution)/shard_map/while/body/eval_jaxpr/dot_general | solution.py:75
  102.9 4.5 %fusion.109 = f32[256,224]{0,1:T(8,128)S(1)} fusion(f32[4096,224]{0,1:T(8,128)} %bitcast.101, s32[4096]{0:T(1024)S(1)} %get-tuple-element.581, f32[256,224]{0,1:T(8,128)S(1)} %get-tuple-element.604, pred[]{:T(512)S(6)} %compare.42), kind=kOutput, calls=%fused_computation.48.clone.1 | convolution fusion | flops 2819735552 | bytes 4145153 | tf_op jit(solution)/shard_map/while/body/eval_jaxpr/dot_general | solution.py:75
  109.9 4.5 %fusion.109 = f32[256,224]{0,1:T(8,128)S(1)} fusion(f32[4096,224]{0,1:T(8,128)} %bitcast.101, s32[4096]{0:T(1024)S(1)} %get-tuple-element.581, f32[256,224]{0,1:T(8,128)S(1)} %get-tuple-element.604, pred[]{:T(512)S(6)} %compare.42), kind=kOutput, calls=%fused_computation.48.clone.1 | convolution fusion | flops 2819735552 | bytes 4145153 | tf_op jit(solution)/shard_map/while/body/eval_jaxpr/dot_general | solution.py:75
  116.9 4.5 %fusion.109 = f32[256,224]{0,1:T(8,128)S(1)} fusion(f32[4096,224]{0,1:T(8,128)} %bitcast.101, s32[4096]{0:T(1024)S(1)} %get-tuple-element.581, f32[256,224]{0,1:T(8,128)S(1)} %get-tuple-element.604, pred[]{:T(512)S(6)} %compare.42), kind=kOutput, calls=%fused_computation.48.clone.1 | convolution fusion | flops 2819735552 | bytes 4145153 | tf_op jit(solution)/shard_map/while/body/eval_jaxpr/dot_general | solution.py:75
  123.9 4.5 %fusion.109 = f32[256,224]{0,1:T(8,128)S(1)} fusion(f32[4096,224]{0,1:T(8,128)} %bitcast.101, s32[4096]{0:T(1024)S(1)} %get-tuple-element.581, f32[256,224]{0,1:T(8,128)S(1)} %get-tuple-element.604, pred[]{:T(512)S(6)} %compare.42), kind=kOutput, calls=%fused_computation.48.clone.1 | convolution fusion | flops 2819735552 | bytes 4145153 | tf_op jit(solution)/shard_map/while/body/eval_jaxpr/dot_general | solution.py:75
  130.9 4.5 %fusion.109 = f32[256,224]{0,1:T(8,128)S(1)} fusion(f32[4096,224]{0,1:T(8,128)} %bitcast.101, s32[4096]{0:T(1024)S(1)} %get-tuple-element.581, f32[256,224]{0,1:T(8,128)S(1)} %get-tuple-element.604, pred[]{:T(512)S(6)} %compare.42), kind=kOutput, calls=%fused_computation.48.clone.1 | convolution fusion | flops 2819735552 | bytes 4145153 | tf_op jit(solution)/shard_map/while/body/eval_jaxpr/dot_general | solution.py:75
  137.9 4.5 %fusion.109 = f32[256,224]{0,1:T(8,128)S(1)} fusion(f32[4096,224]{0,1:T(8,128)} %bitcast.101, s32[4096]{0:T(1024)S(1)} %get-tuple-element.581, f32[256,224]{0,1:T(8,128)S(1)} %get-tuple-element.604, pred[]{:T(512)S(6)} %compare.42), kind=kOutput, calls=%fused_computation.48.clone.1 | convolution fusion | flops 2819735552 | bytes 4145153 | tf_op jit(solution)/shard_map/while/body/eval_jaxpr/dot_general | solution.py:75
  144.9 4.5 %fusion.109 = f32[256,224]{0,1:T(8,128)S(1)} fusion(f32[4096,224]{0,1:T(8,128)} %bitcast.101, s32[4096]{0:T(1024)S(1)} %get-tuple-element.581, f32[256,224]{0,1:T(8,128)S(1)} %get-tuple-element.604, pred[]{:T(512)S(6)} %compare.42), kind=kOutput, calls=%fused_computation.48.clone.1 | convolution fusion | flops 2819735552 | bytes 4145153 | tf_op jit(solution)/shard_map/while/body/eval_jaxpr/dot_general | solution.py:75
  151.9 4.5 %fusion.109 = f32[256,224]{0,1:T(8,128)S(1)} fusion(f32[4096,224]{0,1:T(8,128)} %bitcast.101, s32[4096]{0:T(1024)S(1)} %get-tuple-element.581, f32[256,224]{0,1:T(8,128)S(1)} %get-tuple-element.604, pred[]{:T(512)S(6)} %compare.42), kind=kOutput, calls=%fused_computation.48.clone.1 | convolution fusion | flops 2819735552 | bytes 4145153 | tf_op jit(solution)/shard_map/while/body/eval_jaxpr/dot_general | solution.py:75
  158.9 4.5 %fusion.109 = f32[256,224]{0,1:T(8,128)S(1)} fusion(f32[4096,224]{0,1:T(8,128)} %bitcast.101, s32[4096]{0:T(1024)S(1)} %get-tuple-element.581, f32[256,224]{0,1:T(8,128)S(1)} %get-tuple-element.604, pred[]{:T(512)S(6)} %compare.42), kind=kOutput, calls=%fused_computation.48.clone.1 | convolution fusion | flops 2819735552 | bytes 4145153 | tf_op jit(solution)/shard_map/while/body/eval_jaxpr/dot_general | solution.py:75
  165.9 4.5 %fusion.109 = f32[256,224]{0,1:T(8,128)S(1)} fusion(f32[4096,224]{0,1:T(8,128)} %bitcast.101, s32[4096]{0:T(1024)S(1)} %get-tuple-element.581, f32[256,224]{0,1:T(8,128)S(1)} %get-tuple-element.604, pred[]{:T(512)S(6)} %compare.42), kind=kOutput, calls=%fused_computation.48.clone.1 | convolution fusion | flops 2819735552 | bytes 4145153 | tf_op jit(solution)/shard_map/while/body/eval_jaxpr/dot_general | solution.py:75
  193.9 4.5 %fusion.109 = f32[256,224]{0,1:T(8,128)S(1)} fusion(f32[4096,224]{0,1:T(8,128)} %bitcast.101, s32[4096]{0:T(1024)S(1)} %get-tuple-element.581, f32[256,224]{0,1:T(8,128)S(1)} %get-tuple-element.604, pred[]{:T(512)S(6)} %compare.42), kind=kOutput, calls=%fused_computation.48.clone.1 | convolution fusion | flops 2819735552 | bytes 4145153 | tf_op jit(solution)/shard_map/while/body/eval_jaxpr/dot_general | solution.py:75
  222.5 4.7 %collective-permute-start.5 = (f32[7,1,16,128]{3,2,1,0:T(8,128)S(1)}, f32[7,1,16,128]{3,2,1,0:T(8,128)S(1)}, u32[]{:S(2)}, u32[]{:S(2)}) collective-permute-start(f32[7,1,16,128]{3,2,1,0:T(8,128)S(1)} %get-tuple-element.461), channel_id=1, source_target_pairs={{0,16},{16,32},{32,48},{48,64},{64,80},{80,96},{96,112},{1,17},{17... | collective-permute-start | bytes 172040 | tf_op jit(solution)/shard_map/ppermute | solution.py:18
  229.8 4.6 %collective-permute-start.7 = (f32[7,6,1,128]{3,2,1,0:T(1,128)S(1)}, f32[7,6,1,128]{3,2,1,0:T(1,128)S(1)}, u32[]{:S(2)}, u32[]{:S(2)}) collective-permute-start(f32[7,6,1,128]{3,2,1,0:T(1,128)S(1)} %get-tuple-element.448), channel_id=1, source_target_pairs={{0,1},{1,2},{2,3},{3,4},{4,5},{5,6},{6,7},{7,8},{8,9},{9,10},{10,1... | collective-permute-start | bytes 64520 | tf_op jit(solution)/shard_map/ppermute | solution.py:18
  237.4 5.1 %collective-permute-start.9 = (f32[7,1,16,128]{3,2,1,0:T(8,128)S(1)}, f32[7,1,16,128]{3,2,1,0:T(8,128)S(1)}, u32[]{:S(2)}, u32[]{:S(2)}) collective-permute-start(f32[7,1,16,128]{3,2,1,0:T(8,128)S(1)} %get-tuple-element.459), channel_id=1, source_target_pairs={{0,16},{16,32},{32,48},{48,64},{64,80},{80,96},{96,112},{1,17},{17... | collective-permute-start | bytes 172040 | tf_op jit(solution)/shard_map/ppermute | solution.py:18
  245.1 4.6 %collective-permute-start.11 = (f32[7,6,1,128]{3,2,1,0:T(1,128)S(1)}, f32[7,6,1,128]{3,2,1,0:T(1,128)S(1)}, u32[]{:S(2)}, u32[]{:S(2)}) collective-permute-start(f32[7,6,1,128]{3,2,1,0:T(1,128)S(1)} %get-tuple-element.446), channel_id=1, source_target_pairs={{0,1},{1,2},{2,3},{3,4},{4,5},{5,6},{6,7},{7,8},{8,9},{9,10},{10,1... | collective-permute-start | bytes 64520 | tf_op jit(solution)/shard_map/ppermute | solution.py:18
  252.7 5.1 %collective-permute-start.13 = (f32[7,1,16,128]{3,2,1,0:T(8,128)S(1)}, f32[7,1,16,128]{3,2,1,0:T(8,128)S(1)}, u32[]{:S(2)}, u32[]{:S(2)}) collective-permute-start(f32[7,1,16,128]{3,2,1,0:T(8,128)S(1)} %get-tuple-element.457), channel_id=1, source_target_pairs={{0,16},{16,32},{32,48},{48,64},{64,80},{80,96},{96,112},{1,17},{17... | collective-permute-start | bytes 172040 | tf_op jit(solution)/shard_map/ppermute | solution.py:18
  260.4 4.6 %collective-permute-start.15 = (f32[7,6,1,128]{3,2,1,0:T(1,128)S(1)}, f32[7,6,1,128]{3,2,1,0:T(1,128)S(1)}, u32[]{:S(2)}, u32[]{:S(2)}) collective-permute-start(f32[7,6,1,128]{3,2,1,0:T(1,128)S(1)} %get-tuple-element.444), channel_id=1, source_target_pairs={{0,1},{1,2},{2,3},{3,4},{4,5},{5,6},{6,7},{7,8},{8,9},{9,10},{10,1... | collective-permute-start | bytes 64520 | tf_op jit(solution)/shard_map/ppermute | solution.py:18
  273.4 17.1 %all-to-all-start.1 = ((f32[128,1,192]{2,1,0:T(1,128)}), f32[128,1,192]{2,1,0:T(1,128)S(1)}, u32[]{:S(2)}, u32[]{:S(2)}) async-start(f32[128,1,192]{2,1,0:T(1,128)} %reshape.600), calls=%async_computation.1 | async-start | bytes 262144 | tf_op jit(solution)/shard_map/all_to_all | solution.py:135
  291.2 9.5 %all-to-all-done.1 = f32[128,1,192]{2,1,0:T(1,128)S(1)} async-done(((f32[128,1,192]{2,1,0:T(1,128)}), f32[128,1,192]{2,1,0:T(1,128)S(1)}, u32[]{:S(2)}, u32[]{:S(2)}) %all-to-all-start.1) | async-done | bytes 98336 | tf_op jit(solution)/shard_map/all_to_all | solution.py:135
  (324 shorter events, 162.9 us)
Async XLA Ops:
  44.2 1.7 copy-start.2
  48.6 11.5 %copy-start.3 = (s32[65536]{0:T(1024)S(1)}, s32[65536]{0:T(1024)}, u32[]{:S(2)}) copy-start(s32[65536]{0:T(1024)} %param.18) | copy-start | bytes 786436
  48.6 11.6 %copy-start = (f32[4,16,128]{2,1,0:T(8,128)S(1)}, f32[4,16,128]{2,1,0:T(8,128)}, u32[]{:S(2)}) copy-start(f32[4,16,128]{2,1,0:T(8,128)} %param.19) | copy-start | bytes 98308
  48.7 40.8 %all-to-all-start = ((f32[7,128,512]{2,0,1:T(8,128)}), f32[7,128,512]{2,0,1:T(8,128)S(1)}, u32[]{:S(2)}, u32[]{:S(2)}) async-start(f32[7,128,512]{2,0,1:T(8,128)} %copy.42), calls=%async_computation | async-start | bytes 4194304 | tf_op jit(solution)/shard_map/all_to_all | solution.py:111
  206.1 5.9 %collective-permute-start = (f32[7,1,16,128]{3,2,1,0:T(8,128)S(1)}, f32[7,1,16,128]{3,2,1,0:T(8,128)S(1)}, u32[]{:S(2)}, u32[]{:S(2)}) collective-permute-start(f32[7,1,16,128]{3,2,1,0:T(8,128)S(1)} %get-tuple-element.464), channel_id=1, source_target_pairs={{16,0},{32,16},{48,32},{64,48},{80,64},{96,80},{112,96},{17,1},{33... | collective-permute-start | bytes 172040 | tf_op jit(solution)/shard_map/ppermute | solution.py:19
  209.5 3.7 %collective-permute-start.1 = (f32[7,1,16,128]{3,2,1,0:T(8,128)S(1)}, f32[7,1,16,128]{3,2,1,0:T(8,128)S(1)}, u32[]{:S(2)}, u32[]{:S(2)}) collective-permute-start(f32[7,1,16,128]{3,2,1,0:T(8,128)S(1)} %get-tuple-element.463), channel_id=1, source_target_pairs={{0,16},{16,32},{32,48},{48,64},{64,80},{80,96},{96,112},{1,17},{17... | collective-permute-start | bytes 172040 | tf_op jit(solution)/shard_map/ppermute | solution.py:18
  213.2 5.3 %collective-permute-start.2 = (f32[7,6,1,128]{3,2,1,0:T(1,128)S(1)}, f32[7,6,1,128]{3,2,1,0:T(1,128)S(1)}, u32[]{:S(2)}, u32[]{:S(2)}) collective-permute-start(f32[7,6,1,128]{3,2,1,0:T(1,128)S(1)} %get-tuple-element.449), channel_id=1, source_target_pairs={{1,0},{2,1},{3,2},{4,3},{5,4},{6,5},{7,6},{8,7},{9,8},{10,9},{11,1... | collective-permute-start | bytes 64520 | tf_op jit(solution)/shard_map/ppermute | solution.py:19
  214.5 4.9 %collective-permute-start.3 = (f32[7,6,1,128]{3,2,1,0:T(1,128)S(1)}, f32[7,6,1,128]{3,2,1,0:T(1,128)S(1)}, u32[]{:S(2)}, u32[]{:S(2)}) collective-permute-start(f32[7,6,1,128]{3,2,1,0:T(1,128)S(1)} %get-tuple-element.450), channel_id=1, source_target_pairs={{0,1},{1,2},{2,3},{3,4},{4,5},{5,6},{6,7},{7,8},{8,9},{9,10},{10,1... | collective-permute-start | bytes 64520 | tf_op jit(solution)/shard_map/ppermute | solution.py:18
  219.7 7.5 %collective-permute-start.4 = (f32[7,1,16,128]{3,2,1,0:T(8,128)S(1)}, f32[7,1,16,128]{3,2,1,0:T(8,128)S(1)}, u32[]{:S(2)}, u32[]{:S(2)}) collective-permute-start(f32[7,1,16,128]{3,2,1,0:T(8,128)S(1)} %get-tuple-element.462), channel_id=1, source_target_pairs={{16,0},{32,16},{48,32},{64,48},{80,64},{96,80},{112,96},{17,1},{33... | collective-permute-start | bytes 172040 | tf_op jit(solution)/shard_map/ppermute | solution.py:19
  222.5 5.9 %collective-permute-start.5 = (f32[7,1,16,128]{3,2,1,0:T(8,128)S(1)}, f32[7,1,16,128]{3,2,1,0:T(8,128)S(1)}, u32[]{:S(2)}, u32[]{:S(2)}) collective-permute-start(f32[7,1,16,128]{3,2,1,0:T(8,128)S(1)} %get-tuple-element.461), channel_id=1, source_target_pairs={{0,16},{16,32},{32,48},{48,64},{64,80},{80,96},{96,112},{1,17},{17... | collective-permute-start | bytes 172040 | tf_op jit(solution)/shard_map/ppermute | solution.py:18
  228.5 37.1 %copy-start.5 = (s32[1,8192]{1,0:T(1,128)S(1)}, s32[1,8192]{1,0:T(1,128)}, u32[]{:S(2)}) copy-start(s32[1,8192]{1,0:T(1,128)} %param.20) | copy-start | bytes 98308
  228.5 5.9 %collective-permute-start.6 = (f32[7,6,1,128]{3,2,1,0:T(1,128)S(1)}, f32[7,6,1,128]{3,2,1,0:T(1,128)S(1)}, u32[]{:S(2)}, u32[]{:S(2)}) collective-permute-start(f32[7,6,1,128]{3,2,1,0:T(1,128)S(1)} %get-tuple-element.447), channel_id=1, source_target_pairs={{1,0},{2,1},{3,2},{4,3},{5,4},{6,5},{7,6},{8,7},{9,8},{10,9},{11,1... | collective-permute-start | bytes 64520 | tf_op jit(solution)/shard_map/ppermute | solution.py:19
  229.8 5.5 %collective-permute-start.7 = (f32[7,6,1,128]{3,2,1,0:T(1,128)S(1)}, f32[7,6,1,128]{3,2,1,0:T(1,128)S(1)}, u32[]{:S(2)}, u32[]{:S(2)}) collective-permute-start(f32[7,6,1,128]{3,2,1,0:T(1,128)S(1)} %get-tuple-element.448), channel_id=1, source_target_pairs={{0,1},{1,2},{2,3},{3,4},{4,5},{5,6},{6,7},{7,8},{8,9},{9,10},{10,1... | collective-permute-start | bytes 64520 | tf_op jit(solution)/shard_map/ppermute | solution.py:18
  235.5 7.0 %collective-permute-start.8 = (f32[7,1,16,128]{3,2,1,0:T(8,128)S(1)}, f32[7,1,16,128]{3,2,1,0:T(8,128)S(1)}, u32[]{:S(2)}, u32[]{:S(2)}) collective-permute-start(f32[7,1,16,128]{3,2,1,0:T(8,128)S(1)} %get-tuple-element.460), channel_id=1, source_target_pairs={{16,0},{32,16},{48,32},{64,48},{80,64},{96,80},{112,96},{17,1},{33... | collective-permute-start | bytes 172040 | tf_op jit(solution)/shard_map/ppermute | solution.py:19
  237.4 6.4 %collective-permute-start.9 = (f32[7,1,16,128]{3,2,1,0:T(8,128)S(1)}, f32[7,1,16,128]{3,2,1,0:T(8,128)S(1)}, u32[]{:S(2)}, u32[]{:S(2)}) collective-permute-start(f32[7,1,16,128]{3,2,1,0:T(8,128)S(1)} %get-tuple-element.459), channel_id=1, source_target_pairs={{0,16},{16,32},{32,48},{48,64},{64,80},{80,96},{96,112},{1,17},{17... | collective-permute-start | bytes 172040 | tf_op jit(solution)/shard_map/ppermute | solution.py:18
  243.8 5.9 %collective-permute-start.10 = (f32[7,6,1,128]{3,2,1,0:T(1,128)S(1)}, f32[7,6,1,128]{3,2,1,0:T(1,128)S(1)}, u32[]{:S(2)}, u32[]{:S(2)}) collective-permute-start(f32[7,6,1,128]{3,2,1,0:T(1,128)S(1)} %get-tuple-element.445), channel_id=1, source_target_pairs={{1,0},{2,1},{3,2},{4,3},{5,4},{6,5},{7,6},{8,7},{9,8},{10,9},{11,1... | collective-permute-start | bytes 64520 | tf_op jit(solution)/shard_map/ppermute | solution.py:19
  245.1 5.5 %collective-permute-start.11 = (f32[7,6,1,128]{3,2,1,0:T(1,128)S(1)}, f32[7,6,1,128]{3,2,1,0:T(1,128)S(1)}, u32[]{:S(2)}, u32[]{:S(2)}) collective-permute-start(f32[7,6,1,128]{3,2,1,0:T(1,128)S(1)} %get-tuple-element.446), channel_id=1, source_target_pairs={{0,1},{1,2},{2,3},{3,4},{4,5},{5,6},{6,7},{7,8},{8,9},{9,10},{10,1... | collective-permute-start | bytes 64520 | tf_op jit(solution)/shard_map/ppermute | solution.py:18
  250.8 7.0 %collective-permute-start.12 = (f32[7,1,16,128]{3,2,1,0:T(8,128)S(1)}, f32[7,1,16,128]{3,2,1,0:T(8,128)S(1)}, u32[]{:S(2)}, u32[]{:S(2)}) collective-permute-start(f32[7,1,16,128]{3,2,1,0:T(8,128)S(1)} %get-tuple-element.458), channel_id=1, source_target_pairs={{16,0},{32,16},{48,32},{64,48},{80,64},{96,80},{112,96},{17,1},{33... | collective-permute-start | bytes 172040 | tf_op jit(solution)/shard_map/ppermute | solution.py:19
  252.7 6.4 %collective-permute-start.13 = (f32[7,1,16,128]{3,2,1,0:T(8,128)S(1)}, f32[7,1,16,128]{3,2,1,0:T(8,128)S(1)}, u32[]{:S(2)}, u32[]{:S(2)}) collective-permute-start(f32[7,1,16,128]{3,2,1,0:T(8,128)S(1)} %get-tuple-element.457), channel_id=1, source_target_pairs={{0,16},{16,32},{32,48},{48,64},{64,80},{80,96},{96,112},{1,17},{17... | collective-permute-start | bytes 172040 | tf_op jit(solution)/shard_map/ppermute | solution.py:18
  259.1 7.1 %collective-permute-start.14 = (f32[7,6,1,128]{3,2,1,0:T(1,128)S(1)}, f32[7,6,1,128]{3,2,1,0:T(1,128)S(1)}, u32[]{:S(2)}, u32[]{:S(2)}) collective-permute-start(f32[7,6,1,128]{3,2,1,0:T(1,128)S(1)} %get-tuple-element.443), channel_id=1, source_target_pairs={{1,0},{2,1},{3,2},{4,3},{5,4},{6,5},{7,6},{8,7},{9,8},{10,9},{11,1... | collective-permute-start | bytes 64520 | tf_op jit(solution)/shard_map/ppermute | solution.py:19
  260.4 5.8 %collective-permute-start.15 = (f32[7,6,1,128]{3,2,1,0:T(1,128)S(1)}, f32[7,6,1,128]{3,2,1,0:T(1,128)S(1)}, u32[]{:S(2)}, u32[]{:S(2)}) collective-permute-start(f32[7,6,1,128]{3,2,1,0:T(1,128)S(1)} %get-tuple-element.444), channel_id=1, source_target_pairs={{0,1},{1,2},{2,3},{3,4},{4,5},{5,6},{6,7},{7,8},{8,9},{9,10},{10,1... | collective-permute-start | bytes 64520 | tf_op jit(solution)/shard_map/ppermute | solution.py:18
  266.6 1.2 copy-start.1
  267.8 22.7 %copy-start.6 = (s32[1,8192]{1,0:T(1,128)S(1)}, s32[1,8192]{1,0:T(1,128)}, u32[]{:S(2)}) copy-start(s32[1,8192]{1,0:T(1,128)} %param.21) | copy-start | bytes 98308
  273.4 27.3 %all-to-all-start.1 = ((f32[128,1,192]{2,1,0:T(1,128)}), f32[128,1,192]{2,1,0:T(1,128)S(1)}, u32[]{:S(2)}, u32[]{:S(2)}) async-start(f32[128,1,192]{2,1,0:T(1,128)} %reshape.600), calls=%async_computation.1 | async-start | bytes 262144 | tf_op jit(solution)/shard_map/all_to_all | solution.py:135
  (1 other events, 0.7 us)
where the time goes:
time: 309 us; the launch traced here: 308 us
  matrix products  105 us (34%)
  starting transfers between devices  78.8 us (26%)
  other arithmetic  53.5 us (17%)
  waiting for transfers between devices  46.2 us (15%)
  local copies, waits for them, and re-layouts  21.1 us (7%)
    dot_general x16, matrix products, add_block(): lax.dot_general(onehot, spread, (((0,), (0,)), ((), ())), precision=lax.P...  72.1 us
    mul x16, other arithmetic, add_block(): spread = (vals.T[:, :, None] * lanes[:, None, :]).reshape(block, rows * 32)  35.2 us
    ppermute x8, starting transfers between devices, padded_2(): before = lax.ppermute(last, axis, up)  35 us
    dot_general x20, matrix products, one_block(): jnp.dot(folded, onehot, precision=lax.Precision.HIGHEST, preferred_elemen...  32.5 us
    all_to_all x1, waiting for transfers between devices, on_device(): lax.all_to_all(values, ('src', 'tgt'), split_axis=1, concat_axis=1, tiled...  29.1 us
    all_to_all x1, starting transfers between devices, on_device(): lax.all_to_all(outgoing.reshape(rows, owners, quota), ('src', 'tgt'), spl...  17.1 us
    ppermute x8, starting transfers between devices, padded_2(): after = lax.ppermute(first, axis, down)  15.3 us
    all_to_all x1, starting transfers between devices, on_device(): lax.all_to_all(values, ('src', 'tgt'), split_axis=1, concat_axis=1, tiled...  11.5 us
  transfers between devices with their start and end apart: 18, of which 9 were waited for; matrix products, arithmetic and copies ran while one was open for 1% of the time, Pallas kernels for 0%

commit v1 on v0

--- a/solution.py
+++ b/solution.py
@@ -1,11 +1,240 @@
+import functools
 import math
 
 import jax
 import jax.numpy as jnp
 from jax import lax
+from jax.experimental import pallas as pl
+from jax.experimental.pallas import tpu as pltpu
 from jax.sharding import PartitionSpec as P
 
 ITERS = 4
+MESH = pl.DeviceIdType.MESH
+STEP = 2
+AHEAD = 8
+
+
+def gather_pair(fields, source, weight, pair, store):
+    rows = pl.ds(pl.multiple_of(8 * pair, 8), 8)
+    index = source[rows, :]
+    wgt = weight[rows, :]
+    lane = index & 127
+    group = index >> 7
+    bits = [(group & (1 << b)) != 0 for b in range(5)]
+    for f in range(7):
+        vals = [
+            jnp.take_along_axis(
+                jnp.broadcast_to(fields[f : f + 1, 128 * r : 128 * r + 128], (8, 128)),
+                lane,
+                axis=1,
+                mode="promise_in_bounds",
+            )
+            for r in range(32)
+        ]
+        for bit in bits:
+            vals = [jnp.where(bit, vals[2 * j + 1], vals[2 * j]) for j in range(len(vals) // 2)]
+        store(f, vals[0] * wgt)
+
+
+def scatter_pairs(arrived, target, total, pairs):
+    iota = lax.broadcasted_iota(jnp.int32, (16, 128), 0).astype(jnp.int16)
+    one = jnp.ones((16, 128), jnp.bfloat16)
+    zero = jnp.zeros((16, 128), jnp.bfloat16)
+    columns, values = [], []
+    for slot, pair in pairs:
+        for row in range(8):
+            half, r = divmod(row, 4)
+            cell = jnp.broadcast_to(target[pl.ds(8 * pair + row, 1), :], (16, 128))
+            x = cell >> 11
+            col = (((x & 1) << 7) + (cell & 127)).astype(jnp.int16)
+            up = (((x >> 1) << 4) + ((cell >> 7) & 15)).astype(jnp.int16)
+            columns.append(
+                jnp.concatenate(
+                    [jnp.where(iota == col - jnp.int16(16 * i), one, zero) for i in range(16)], axis=0
+                )
+            )
+            here = [iota == up - jnp.int16(16 * i) for i in range(2)]
+            high, low = [], []
+            for f in range(7):
+                val = jnp.broadcast_to(arrived[2 * slot + half, f, r : r + 1, :], (16, 128))
+                top = val.astype(jnp.bfloat16)
+                rest = (val - top.astype(jnp.float32)).astype(jnp.bfloat16)
+                high += [jnp.where(m, top, zero) for m in here]
+                low += [jnp.where(m, rest, zero) for m in here]
+            values.append(jnp.concatenate(high + low, axis=0))
+    total[...] += lax.dot_general(
+        jnp.concatenate(values, axis=1),
+        jnp.concatenate(columns, axis=1),
+        (((1,), (1,)), ((), ())),
+        preferred_element_type=jnp.float32,
+    )
+
+
+def project_kernel(
+    n_src, n_tgt, fields, source, weight, target, rhs, outgoing, arrived, total, send_sem, recv_sem
+):
+    owners = n_src * n_tgt
+    pairs = owners // 2
+    steps = pairs // STEP
+    me = lax.axis_index("src") * n_tgt + lax.axis_index("tgt")
+    my_pair, parity = me // 2, me % 2
+
+    barrier = pltpu.get_barrier_semaphore()
+
+    def greet(k):
+        other = (me + k) % owners
+        pl.semaphore_signal(
+            barrier, inc=1, device_id=(other // n_tgt, other % n_tgt), device_id_type=MESH
+        )
+
+    def gather(k):
+        for u in range(STEP):
+            slot = STEP * k + u
+
+            def store(f, val):
+                outgoing[2 * slot, f] = val[:4]
+                outgoing[2 * slot + 1, f] = val[4:]
+
+            gather_pair(fields, source, weight, (my_pair + slot) % pairs, store)
+
+    def copy(slot, half):
+        other = 2 * ((my_pair + slot) % pairs) + half
+        return pltpu.make_async_remote_copy(
+            src_ref=outgoing.at[2 * slot + half],
+            dst_ref=arrived.at[2 * slot + parity],
+            send_sem=send_sem.at[2 * slot + half],
+            recv_sem=recv_sem.at[2 * slot + parity],
+            device_id=(other // n_tgt, other % n_tgt),
+            device_id_type=MESH,
+        )
+
+    def incoming(slot, half):
+        other = 2 * ((my_pair + slot) % pairs) + half
+        return pltpu.make_async_remote_copy(
+            src_ref=outgoing.at[2 * slot + half],
+            dst_ref=arrived.at[2 * slot + half],
+            send_sem=send_sem.at[2 * slot + half],
+            recv_sem=recv_sem.at[2 * slot + half],
+            device_id=(other // n_tgt, other % n_tgt),
+            device_id_type=MESH,
+        )
+
+    def first(k, carry):
+        @pl.when(k > 0)
+        def _():
+            greet_base = k * (owners // AHEAD)
+            for i in range(owners // AHEAD):
+                greet(greet_base + i)
+
+        @pl.when(k == 0)
+        def _():
+            for i in range(1, owners // AHEAD):
+                greet(i)
+
+        gather(k)
+        return carry
+
+    def launch(k):
+        for u in range(STEP):
+            for half in range(2):
+                copy(STEP * k + u, half).start()
+
+    def take(k):
+        for u in range(STEP):
+            for half in range(2):
+                incoming(STEP * k + u, half).wait_recv()
+
+    def scatter(k):
+        scatter_pairs(
+            arrived,
+            target,
+            total,
+            [(STEP * k + u, (my_pair - STEP * k - u + pairs) % pairs) for u in range(STEP)],
+        )
+
+    total[...] = jnp.zeros_like(total)
+    lax.fori_loop(0, AHEAD, first, 0)
+    pl.semaphore_wait(barrier, owners - 1)
+
+    copy(0, 1 - parity).start()
+    for u in range(1, STEP):
+        for half in range(2):
+            copy(u, half).start()
+    arrived[parity] = outgoing[parity]
+
+    def launch_only(k, carry):
+        launch(k)
+        return carry
+
+    lax.fori_loop(1, AHEAD, launch_only, 0)
+
+    incoming(0, 1 - parity).wait_recv()
+    for u in range(1, STEP):
+        for half in range(2):
+            incoming(u, half).wait_recv()
+    gather(AHEAD)
+    scatter(0)
+    launch(AHEAD)
+
+    def both(k, carry):
+        take(k)
+        gather(k + AHEAD)
+        scatter(k)
+        launch(k + AHEAD)
+        return carry
+
+    lax.fori_loop(1, steps - AHEAD, both, 0)
+
+    def last(k, carry):
+        take(k)
+        scatter(k)
+        return carry
+
+    lax.fori_loop(steps - AHEAD, steps, last, 0)
+
+    for f in range(7):
+        for x in range(4):
+            rows = pl.ds(32 * f + 16 * (x // 2), 16)
+            lower = pl.ds(224 + 32 * f + 16 * (x // 2), 16)
+            cols = pl.ds(128 * (x % 2), 128)
+            rhs[f, x] = total[rows, cols] + total[lower, cols]
+
+    copy(0, 1 - parity).wait_send()
+
+    def drain(k, carry):
+        for half in range(2):
+            copy(k, half).wait_send()
+        return carry
+
+    lax.fori_loop(1, pairs, drain, 0)
+
+
+def project(source_fields, slot_source, slot_weight, slot_target):
+    n_src = lax.axis_size("src")
+    n_tgt = lax.axis_size("tgt")
+    owners = n_src * n_tgt
+    vmem = pl.BlockSpec(memory_space=pltpu.VMEM)
+    return pl.pallas_call(
+        functools.partial(project_kernel, n_src, n_tgt),
+        out_shape=jax.ShapeDtypeStruct((7, 4, 16, 128), jnp.float32),
+        in_specs=[vmem] * 4,
+        out_specs=vmem,
+        scratch_shapes=[
+            pltpu.VMEM((owners, 7, 4, 128), jnp.float32),
+            pltpu.VMEM((owners, 7, 4, 128), jnp.float32),
+            pltpu.VMEM((448, 256), jnp.float32),
+            pltpu.SemaphoreType.DMA((owners,)),
+            pltpu.SemaphoreType.DMA((owners,)),
+        ],
+        compiler_params=pltpu.CompilerParams(
+            collective_id=0, has_side_effects=True, vmem_limit_bytes=48 << 20
+        ),
+    )(
+        source_fields,
+        slot_source.reshape(4 * owners, 128),
+        slot_weight.reshape(4 * owners, 128),
+        slot_target.reshape(4 * owners, 128),
+    )
 
 
 def padded_2(x, sides, width):
@@ -57,35 +286,6 @@
     return pieces.transpose(1, 0, 2).reshape(rows, count)
 
 
-def spread_columns(values, index, width):
-    rows, count = values.shape
-    groups = width // 32
-    block = math.gcd(count, 4096)
-    blocks = count // block
-    group_ids = jnp.arange(groups, dtype=jnp.int32)
-    lane_ids = jnp.arange(32, dtype=jnp.int32)
-    value_blocks = values.reshape(rows, blocks, block).transpose(1, 0, 2)
-    index_blocks = index.reshape(blocks, block)
-
-    def add_block(total, inputs):
-        vals, piece = inputs
-        onehot = (piece[:, None] // 32 == group_ids[None, :]).astype(jnp.float32)
-        lanes = (piece[:, None] % 32 == lane_ids[None, :]).astype(jnp.float32)
-        spread = (vals.T[:, :, None] * lanes[:, None, :]).reshape(block, rows * 32)
-        added = lax.dot_general(
-            onehot,
-            spread,
-            (((0,), (0,)), ((), ())),
-            precision=lax.Precision.HIGHEST,
-            preferred_element_type=jnp.float32,
-        )
-        return (total + added, None)
-
-    start = jnp.zeros((groups, rows * 32), jnp.float32)
-    total, _ = lax.scan(add_block, start, (value_blocks, index_blocks))
-    return total.reshape(groups, rows, 32).transpose(1, 0, 2).reshape(rows, width)
-
-
 def mass_apply(field, root):
     w = root[None] * field
     padded = padded_2(w, (("src", 1), ("tgt", 2)), 1)
@@ -102,16 +302,10 @@
     n_src = lax.axis_size("src")
     n_tgt = lax.axis_size("tgt")
     owners = n_src * n_tgt
-    per_owner = slot_source.shape[0] // owners
     hx_cells, hy_cells, hz_cells = cell_mass.shape
     cells = hx_cells * hy_cells * hz_cells
     quota = cells // owners
-    values = slot_weight[None, :] * lookup_columns(source_fields, slot_source)
-    values = values.reshape(7, owners, per_owner)
-    arrived = lax.all_to_all(values, ("src", "tgt"), split_axis=1, concat_axis=1, tiled=True)
-    arrived = arrived.reshape(7, owners * per_owner)
-    rhs = spread_columns(arrived, slot_target, cells)
-    rhs = rhs.reshape(7, hx_cells, hy_cells, hz_cells)
+    rhs = project(source_fields, slot_source, slot_weight, slot_target)
     root = jnp.sqrt(cell_mass)
     theta = 1.0
     delta = 0.75

time: 309 us -> 164 us (0.53)
  matrix products: 105 us -> 6.51 us
  Pallas kernels: 0 us -> 51.6 us
  other arithmetic: 53.5 us -> 6.07 us
  waiting for transfers between devices: 46.2 us -> 17 us
  local copies, waits for them, and re-layouts: 21.1 us -> 9.19 us
  starting transfers between devices: 78.8 us -> 71.2 us
    dot_general x16 -> x0, matrix products: 72.1 us -> none  [add_block(): lax.dot_general(onehot, spread, (((0,), (0,)), ((), ())), precision=lax.P...]
    pallas_call x0 -> x1, Pallas kernels: none -> 51.6 us  [project(): pl.pallas_call(functools.partial(project_kernel, n_src, n_tgt), out_shape...]
    mul x17 -> x0, other arithmetic: 35.4 us -> none  [the longest x16 35.2 us: add_block(): spread = (vals.T[:, :, None] * lanes[:, None, :]).reshape(block, rows * 32)]
    all_to_all x1 -> x0, waiting for transfers between devices: 29.1 us -> none  [on_device(): lax.all_to_all(values, ('src', 'tgt'), split_axis=1, concat_axis=1, tiled...]
    dot_general x20 -> x4, matrix products: 32.5 us -> 6.51 us  [one_block(): jnp.dot(folded, onehot, precision=lax.Precision.HIGHEST, preferred_elemen...]
    all_to_all x1 -> x0, starting transfers between devices: 11.5 us -> none  [on_device(): lax.all_to_all(values, ('src', 'tgt'), split_axis=1, concat_axis=1, tiled...]
    reduce_sum x20 -> x4, other arithmetic: 9.92 us -> 1.04 us  [one_block(): return jnp.sum(picked * lanes[None], axis=1)]
    reshape x5 -> x0, local copies, waits for them, and re-layouts: 4.08 us -> none  [the longest x1 1.65 us: lookup_columns(): return pieces.transpose(1, 0, 2).reshape(rows, count)]
  transfers between devices with their start and end apart: 18 -> 17, of which waited for: 9 -> 8; matrix products, arithmetic and copies ran while one was open for 1% -> 1% of each run, Pallas kernels for 0% -> 0%
where the time goes in v1:
time: 164 us; the launch traced here: 163 us
  starting transfers between devices  71.2 us (43%)
  Pallas kernels  51.6 us (31%)
  waiting for transfers between devices  17 us (10%)
  local copies, waits for them, and re-layouts  9.19 us (6%)
  matrix products  6.51 us (4%)
  other arithmetic  6.07 us (4%)
    pallas_call x1, Pallas kernels, project(): pl.pallas_call(functools.partial(project_kernel, n_src, n_tgt), out_shape...  51.6 us
    ppermute x8, starting transfers between devices, padded_2(): before = lax.ppermute(last, axis, up)  37.3 us
    all_to_all x1, starting transfers between devices, on_device(): lax.all_to_all(outgoing.reshape(rows, owners, quota), ('src', 'tgt'), spl...  19.4 us
    ppermute x8, starting transfers between devices, padded_2(): after = lax.ppermute(first, axis, down)  14.6 us
    all_to_all x1, waiting for transfers between devices, on_device(): lax.all_to_all(outgoing.reshape(rows, owners, quota), ('src', 'tgt'), spl...  9.47 us
    ppermute x8, waiting for transfers between devices, padded_2(): before = lax.ppermute(last, axis, up)  7.56 us
    dot_general x4, matrix products, one_block(): jnp.dot(folded, onehot, precision=lax.Precision.HIGHEST, preferred_elemen...  6.51 us
    unnamed x21, local copies, waits for them, and re-layouts  6 us
  transfers between devices with their start and end apart: 17, of which 8 were waited for; matrix products, arithmetic and copies ran while one was open for 1% of the time, Pallas kernels for 0%

profile of v1, /device:TPU:1, one launch (start us, length us, event | category | flops | bytes accessed | tf_op | source)
XLA Modules:
  0.0 163.0 jit_solution(17183053994217346553)
XLA Ops:
  5.2 51.6 %shard_map.86 = f32[7,4,16,128]{3,2,1,0:T(8,128)S(1)} custom-call(f32[7,4096]{1,0:T(8,128)S(1)} %copy-done.3, s32[512,128]{1,0:T(8,128)S(1)} %bitcast.64, f32[512,128]{1,0:T(8,128)S(1)} %bitcast.65, s32[512,128]{1,0:T(8,128)S(1)} %bitcast.66), custom_call_target="tpu_custom_call" | custom-call | tf_op jit(solution)/shard_map/pallas_call | solution.py:217
  57.7 3.6 %collective-permute-start = (f32[7,1,16,128]{3,2,1,0:T(8,128)S(1)}, f32[7,1,16,128]{3,2,1,0:T(8,128)S(1)}, u32[]{:S(2)}, u32[]{:S(2)}) collective-permute-start(f32[7,1,16,128]{3,2,1,0:T(8,128)S(1)} %get-tuple-element.236), channel_id=1, source_target_pairs={{16,0},{32,16},{48,32},{64,48},{80,64},{96,80},{112,96},{17,1},{33... | collective-permute-start | bytes 172040 | tf_op jit(solution)/shard_map/ppermute | solution.py:248
  61.4 4.0 %collective-permute-start.1 = (f32[7,1,16,128]{3,2,1,0:T(8,128)S(1)}, f32[7,1,16,128]{3,2,1,0:T(8,128)S(1)}, u32[]{:S(2)}, u32[]{:S(2)}) collective-permute-start(f32[7,1,16,128]{3,2,1,0:T(8,128)S(1)} %get-tuple-element.235), channel_id=1, source_target_pairs={{0,16},{16,32},{32,48},{48,64},{64,80},{80,96},{96,112},{1,17},{17... | collective-permute-start | bytes 172040 | tf_op jit(solution)/shard_map/ppermute | solution.py:247
  66.6 1.3 collective-permute-start.2
  67.9 4.0 %collective-permute-start.3 = (f32[7,6,1,128]{3,2,1,0:T(1,128)S(1)}, f32[7,6,1,128]{3,2,1,0:T(1,128)S(1)}, u32[]{:S(2)}, u32[]{:S(2)}) collective-permute-start(f32[7,6,1,128]{3,2,1,0:T(1,128)S(1)} %get-tuple-element.222), channel_id=1, source_target_pairs={{0,1},{1,2},{2,3},{3,4},{4,5},{5,6},{6,7},{7,8},{8,9},{9,10},{10,1... | collective-permute-start | bytes 64520 | tf_op jit(solution)/shard_map/ppermute | solution.py:247
  73.1 1.9 %collective-permute-start.4 = (f32[7,1,16,128]{3,2,1,0:T(8,128)S(1)}, f32[7,1,16,128]{3,2,1,0:T(8,128)S(1)}, u32[]{:S(2)}, u32[]{:S(2)}) collective-permute-start(f32[7,1,16,128]{3,2,1,0:T(8,128)S(1)} %get-tuple-element.234), channel_id=1, source_target_pairs={{16,0},{32,16},{48,32},{64,48},{80,64},{96,80},{112,96},{17,1},{33... | collective-permute-start | bytes 172040 | tf_op jit(solution)/shard_map/ppermute | solution.py:248
  75.0 5.4 %collective-permute-start.5 = (f32[7,1,16,128]{3,2,1,0:T(8,128)S(1)}, f32[7,1,16,128]{3,2,1,0:T(8,128)S(1)}, u32[]{:S(2)}, u32[]{:S(2)}) collective-permute-start(f32[7,1,16,128]{3,2,1,0:T(8,128)S(1)} %get-tuple-element.233), channel_id=1, source_target_pairs={{0,16},{16,32},{32,48},{48,64},{64,80},{80,96},{96,112},{1,17},{17... | collective-permute-start | bytes 172040 | tf_op jit(solution)/shard_map/ppermute | solution.py:247
  81.7 1.3 collective-permute-start.6
  83.0 4.6 %collective-permute-start.7 = (f32[7,6,1,128]{3,2,1,0:T(1,128)S(1)}, f32[7,6,1,128]{3,2,1,0:T(1,128)S(1)}, u32[]{:S(2)}, u32[]{:S(2)}) collective-permute-start(f32[7,6,1,128]{3,2,1,0:T(1,128)S(1)} %get-tuple-element.220), channel_id=1, source_target_pairs={{0,1},{1,2},{2,3},{3,4},{4,5},{5,6},{6,7},{7,8},{8,9},{9,10},{10,1... | collective-permute-start | bytes 64520 | tf_op jit(solution)/shard_map/ppermute | solution.py:247
  88.7 1.9 %collective-permute-start.8 = (f32[7,1,16,128]{3,2,1,0:T(8,128)S(1)}, f32[7,1,16,128]{3,2,1,0:T(8,128)S(1)}, u32[]{:S(2)}, u32[]{:S(2)}) collective-permute-start(f32[7,1,16,128]{3,2,1,0:T(8,128)S(1)} %get-tuple-element.232), channel_id=1, source_target_pairs={{16,0},{32,16},{48,32},{64,48},{80,64},{96,80},{112,96},{17,1},{33... | collective-permute-start | bytes 172040 | tf_op jit(solution)/shard_map/ppermute | solution.py:248
  90.6 5.1 %collective-permute-start.9 = (f32[7,1,16,128]{3,2,1,0:T(8,128)S(1)}, f32[7,1,16,128]{3,2,1,0:T(8,128)S(1)}, u32[]{:S(2)}, u32[]{:S(2)}) collective-permute-start(f32[7,1,16,128]{3,2,1,0:T(8,128)S(1)} %get-tuple-element.231), channel_id=1, source_target_pairs={{0,16},{16,32},{32,48},{48,64},{64,80},{80,96},{96,112},{1,17},{17... | collective-permute-start | bytes 172040 | tf_op jit(solution)/shard_map/ppermute | solution.py:247
  97.0 1.3 collective-permute-start.10
  98.3 4.6 %collective-permute-start.11 = (f32[7,6,1,128]{3,2,1,0:T(1,128)S(1)}, f32[7,6,1,128]{3,2,1,0:T(1,128)S(1)}, u32[]{:S(2)}, u32[]{:S(2)}) collective-permute-start(f32[7,6,1,128]{3,2,1,0:T(1,128)S(1)} %get-tuple-element.218), channel_id=1, source_target_pairs={{0,1},{1,2},{2,3},{3,4},{4,5},{5,6},{6,7},{7,8},{8,9},{9,10},{10,1... | collective-permute-start | bytes 64520 | tf_op jit(solution)/shard_map/ppermute | solution.py:247
  104.0 1.9 %collective-permute-start.12 = (f32[7,1,16,128]{3,2,1,0:T(8,128)S(1)}, f32[7,1,16,128]{3,2,1,0:T(8,128)S(1)}, u32[]{:S(2)}, u32[]{:S(2)}) collective-permute-start(f32[7,1,16,128]{3,2,1,0:T(8,128)S(1)} %get-tuple-element.230), channel_id=1, source_target_pairs={{16,0},{32,16},{48,32},{64,48},{80,64},{96,80},{112,96},{17,1},{33... | collective-permute-start | bytes 172040 | tf_op jit(solution)/shard_map/ppermute | solution.py:248
  105.9 5.1 %collective-permute-start.13 = (f32[7,1,16,128]{3,2,1,0:T(8,128)S(1)}, f32[7,1,16,128]{3,2,1,0:T(8,128)S(1)}, u32[]{:S(2)}, u32[]{:S(2)}) collective-permute-start(f32[7,1,16,128]{3,2,1,0:T(8,128)S(1)} %get-tuple-element.229), channel_id=1, source_target_pairs={{0,16},{16,32},{32,48},{48,64},{64,80},{80,96},{96,112},{1,17},{17... | collective-permute-start | bytes 172040 | tf_op jit(solution)/shard_map/ppermute | solution.py:247
  113.6 4.6 %collective-permute-start.15 = (f32[7,6,1,128]{3,2,1,0:T(1,128)S(1)}, f32[7,6,1,128]{3,2,1,0:T(1,128)S(1)}, u32[]{:S(2)}, u32[]{:S(2)}) collective-permute-start(f32[7,6,1,128]{3,2,1,0:T(1,128)S(1)} %get-tuple-element.216), channel_id=1, source_target_pairs={{0,1},{1,2},{2,3},{3,4},{4,5},{5,6},{6,7},{7,8},{8,9},{9,10},{10,1... | collective-permute-start | bytes 64520 | tf_op jit(solution)/shard_map/ppermute | solution.py:247
  121.0 4.3 %while.26 = (s32[]{:T(128)}, f32[2,3,4096]{2,1,0:T(4,128)S(1)}, s32[2,4096]{1,0:T(2,128)S(1)}, f32[96,256]{1,0:T(8,128)S(1)}, s32[]{:T(128)}) while((s32[]{:T(128)}, f32[2,3,4096]{2,1,0:T(4,128)S(1)}, s32[2,4096]{1,0:T(2,128)S(1)}, f32[96,256]{1,0:T(8,128)S(1)}, s32[]{:T(128)}) %tuple.88), condition=%wide.region_2.3_spmd.clone, body=%wide.region_0.2_spmd.clone.sunk | while | flops 1210138624 | bytes 4603977 | solution.py:285
  121.1 1.6 fusion.74
  123.3 1.6 fusion.74
  126.6 19.4 %all-to-all-start = ((f32[128,1,192]{2,1,0:T(1,128)}), f32[128,1,192]{2,1,0:T(1,128)S(1)}, u32[]{:S(2)}, u32[]{:S(2)}) async-start(f32[128,1,192]{2,1,0:T(1,128)} %reshape.408), calls=%async_computation | async-start | bytes 262144 | tf_op jit(solution)/shard_map/all_to_all | solution.py:329
  146.7 9.5 %all-to-all-done = f32[128,1,192]{2,1,0:T(1,128)S(1)} async-done(((f32[128,1,192]{2,1,0:T(1,128)}), f32[128,1,192]{2,1,0:T(1,128)S(1)}, u32[]{:S(2)}, u32[]{:S(2)}) %all-to-all-start) | async-done | bytes 98336 | tf_op jit(solution)/shard_map/all_to_all | solution.py:329
  158.1 4.3 %while.27 = (s32[]{:T(128)}, f32[2,3,4096]{2,1,0:T(4,128)S(1)}, s32[2,4096]{1,0:T(2,128)S(1)}, f32[96,256]{1,0:T(8,128)S(1)}, s32[]{:T(128)}) while((s32[]{:T(128)}, f32[2,3,4096]{2,1,0:T(4,128)S(1)}, s32[2,4096]{1,0:T(2,128)S(1)}, f32[96,256]{1,0:T(8,128)S(1)}, s32[]{:T(128)}) %tuple.89), condition=%wide.region_5.6_spmd.clone, body=%wide.region_3.5_spmd.clone.sunk | while | flops 1210138624 | bytes 4603977 | solution.py:285
  158.2 1.6 fusion.77
  160.4 1.6 fusion.77
  (102 shorter events, 24.1 us)
Async XLA Ops:
  0.6 72.2 %copy-start.4 = (f32[4,16,128]{2,1,0:T(8,128)S(1)}, f32[4,16,128]{2,1,0:T(8,128)}, u32[]{:S(2)}) copy-start(f32[4,16,128]{2,1,0:T(8,128)} %param.15) | copy-start | bytes 98308
  1.5 1.0 copy-start
  2.4 0.9 copy-start.1
  3.4 0.9 copy-start.2
  57.7 7.7 %collective-permute-start = (f32[7,1,16,128]{3,2,1,0:T(8,128)S(1)}, f32[7,1,16,128]{3,2,1,0:T(8,128)S(1)}, u32[]{:S(2)}, u32[]{:S(2)}) collective-permute-start(f32[7,1,16,128]{3,2,1,0:T(8,128)S(1)} %get-tuple-element.236), channel_id=1, source_target_pairs={{16,0},{32,16},{48,32},{64,48},{80,64},{96,80},{112,96},{17,1},{33... | collective-permute-start | bytes 172040 | tf_op jit(solution)/shard_map/ppermute | solution.py:248
  61.4 5.2 %collective-permute-start.1 = (f32[7,1,16,128]{3,2,1,0:T(8,128)S(1)}, f32[7,1,16,128]{3,2,1,0:T(8,128)S(1)}, u32[]{:S(2)}, u32[]{:S(2)}) collective-permute-start(f32[7,1,16,128]{3,2,1,0:T(8,128)S(1)} %get-tuple-element.235), channel_id=1, source_target_pairs={{0,16},{16,32},{32,48},{48,64},{64,80},{80,96},{96,112},{1,17},{17... | collective-permute-start | bytes 172040 | tf_op jit(solution)/shard_map/ppermute | solution.py:247
  66.6 5.3 %collective-permute-start.2 = (f32[7,6,1,128]{3,2,1,0:T(1,128)S(1)}, f32[7,6,1,128]{3,2,1,0:T(1,128)S(1)}, u32[]{:S(2)}, u32[]{:S(2)}) collective-permute-start(f32[7,6,1,128]{3,2,1,0:T(1,128)S(1)} %get-tuple-element.221), channel_id=1, source_target_pairs={{1,0},{2,1},{3,2},{4,3},{5,4},{6,5},{7,6},{8,7},{9,8},{10,9},{11,1... | collective-permute-start | bytes 64520 | tf_op jit(solution)/shard_map/ppermute | solution.py:248
  67.9 4.9 %collective-permute-start.3 = (f32[7,6,1,128]{3,2,1,0:T(1,128)S(1)}, f32[7,6,1,128]{3,2,1,0:T(1,128)S(1)}, u32[]{:S(2)}, u32[]{:S(2)}) collective-permute-start(f32[7,6,1,128]{3,2,1,0:T(1,128)S(1)} %get-tuple-element.222), channel_id=1, source_target_pairs={{0,1},{1,2},{2,3},{3,4},{4,5},{5,6},{6,7},{7,8},{8,9},{9,10},{10,1... | collective-permute-start | bytes 64520 | tf_op jit(solution)/shard_map/ppermute | solution.py:247
  73.1 7.3 %collective-permute-start.4 = (f32[7,1,16,128]{3,2,1,0:T(8,128)S(1)}, f32[7,1,16,128]{3,2,1,0:T(8,128)S(1)}, u32[]{:S(2)}, u32[]{:S(2)}) collective-permute-start(f32[7,1,16,128]{3,2,1,0:T(8,128)S(1)} %get-tuple-element.234), channel_id=1, source_target_pairs={{16,0},{32,16},{48,32},{64,48},{80,64},{96,80},{112,96},{17,1},{33... | collective-permute-start | bytes 172040 | tf_op jit(solution)/shard_map/ppermute | solution.py:248
  75.0 6.6 %collective-permute-start.5 = (f32[7,1,16,128]{3,2,1,0:T(8,128)S(1)}, f32[7,1,16,128]{3,2,1,0:T(8,128)S(1)}, u32[]{:S(2)}, u32[]{:S(2)}) collective-permute-start(f32[7,1,16,128]{3,2,1,0:T(8,128)S(1)} %get-tuple-element.233), channel_id=1, source_target_pairs={{0,16},{16,32},{32,48},{48,64},{64,80},{80,96},{96,112},{1,17},{17... | collective-permute-start | bytes 172040 | tf_op jit(solution)/shard_map/ppermute | solution.py:247
  81.7 5.9 %collective-permute-start.6 = (f32[7,6,1,128]{3,2,1,0:T(1,128)S(1)}, f32[7,6,1,128]{3,2,1,0:T(1,128)S(1)}, u32[]{:S(2)}, u32[]{:S(2)}) collective-permute-start(f32[7,6,1,128]{3,2,1,0:T(1,128)S(1)} %get-tuple-element.219), channel_id=1, source_target_pairs={{1,0},{2,1},{3,2},{4,3},{5,4},{6,5},{7,6},{8,7},{9,8},{10,9},{11,1... | collective-permute-start | bytes 64520 | tf_op jit(solution)/shard_map/ppermute | solution.py:248
  83.0 5.5 %collective-permute-start.7 = (f32[7,6,1,128]{3,2,1,0:T(1,128)S(1)}, f32[7,6,1,128]{3,2,1,0:T(1,128)S(1)}, u32[]{:S(2)}, u32[]{:S(2)}) collective-permute-start(f32[7,6,1,128]{3,2,1,0:T(1,128)S(1)} %get-tuple-element.220), channel_id=1, source_target_pairs={{0,1},{1,2},{2,3},{3,4},{4,5},{5,6},{6,7},{7,8},{8,9},{9,10},{10,1... | collective-permute-start | bytes 64520 | tf_op jit(solution)/shard_map/ppermute | solution.py:247
  88.7 30.1 %copy-start.7 = (s32[1,8192]{1,0:T(1,128)S(1)}, s32[1,8192]{1,0:T(1,128)}, u32[]{:S(2)}) copy-start(s32[1,8192]{1,0:T(1,128)} %param.16) | copy-start | bytes 98308
  88.7 7.0 %collective-permute-start.8 = (f32[7,1,16,128]{3,2,1,0:T(8,128)S(1)}, f32[7,1,16,128]{3,2,1,0:T(8,128)S(1)}, u32[]{:S(2)}, u32[]{:S(2)}) collective-permute-start(f32[7,1,16,128]{3,2,1,0:T(8,128)S(1)} %get-tuple-element.232), channel_id=1, source_target_pairs={{16,0},{32,16},{48,32},{64,48},{80,64},{96,80},{112,96},{17,1},{33... | collective-permute-start | bytes 172040 | tf_op jit(solution)/shard_map/ppermute | solution.py:248
  90.6 6.4 %collective-permute-start.9 = (f32[7,1,16,128]{3,2,1,0:T(8,128)S(1)}, f32[7,1,16,128]{3,2,1,0:T(8,128)S(1)}, u32[]{:S(2)}, u32[]{:S(2)}) collective-permute-start(f32[7,1,16,128]{3,2,1,0:T(8,128)S(1)} %get-tuple-element.231), channel_id=1, source_target_pairs={{0,16},{16,32},{32,48},{48,64},{64,80},{80,96},{96,112},{1,17},{17... | collective-permute-start | bytes 172040 | tf_op jit(solution)/shard_map/ppermute | solution.py:247
  97.0 5.9 %collective-permute-start.10 = (f32[7,6,1,128]{3,2,1,0:T(1,128)S(1)}, f32[7,6,1,128]{3,2,1,0:T(1,128)S(1)}, u32[]{:S(2)}, u32[]{:S(2)}) collective-permute-start(f32[7,6,1,128]{3,2,1,0:T(1,128)S(1)} %get-tuple-element.217), channel_id=1, source_target_pairs={{1,0},{2,1},{3,2},{4,3},{5,4},{6,5},{7,6},{8,7},{9,8},{10,9},{11,1... | collective-permute-start | bytes 64520 | tf_op jit(solution)/shard_map/ppermute | solution.py:248
  98.3 5.5 %collective-permute-start.11 = (f32[7,6,1,128]{3,2,1,0:T(1,128)S(1)}, f32[7,6,1,128]{3,2,1,0:T(1,128)S(1)}, u32[]{:S(2)}, u32[]{:S(2)}) collective-permute-start(f32[7,6,1,128]{3,2,1,0:T(1,128)S(1)} %get-tuple-element.218), channel_id=1, source_target_pairs={{0,1},{1,2},{2,3},{3,4},{4,5},{5,6},{6,7},{7,8},{8,9},{9,10},{10,1... | collective-permute-start | bytes 64520 | tf_op jit(solution)/shard_map/ppermute | solution.py:247
  104.0 7.0 %collective-permute-start.12 = (f32[7,1,16,128]{3,2,1,0:T(8,128)S(1)}, f32[7,1,16,128]{3,2,1,0:T(8,128)S(1)}, u32[]{:S(2)}, u32[]{:S(2)}) collective-permute-start(f32[7,1,16,128]{3,2,1,0:T(8,128)S(1)} %get-tuple-element.230), channel_id=1, source_target_pairs={{16,0},{32,16},{48,32},{64,48},{80,64},{96,80},{112,96},{17,1},{33... | collective-permute-start | bytes 172040 | tf_op jit(solution)/shard_map/ppermute | solution.py:248
  105.9 6.4 %collective-permute-start.13 = (f32[7,1,16,128]{3,2,1,0:T(8,128)S(1)}, f32[7,1,16,128]{3,2,1,0:T(8,128)S(1)}, u32[]{:S(2)}, u32[]{:S(2)}) collective-permute-start(f32[7,1,16,128]{3,2,1,0:T(8,128)S(1)} %get-tuple-element.229), channel_id=1, source_target_pairs={{0,16},{16,32},{32,48},{48,64},{64,80},{80,96},{96,112},{1,17},{17... | collective-permute-start | bytes 172040 | tf_op jit(solution)/shard_map/ppermute | solution.py:247
  112.3 7.1 %collective-permute-start.14 = (f32[7,6,1,128]{3,2,1,0:T(1,128)S(1)}, f32[7,6,1,128]{3,2,1,0:T(1,128)S(1)}, u32[]{:S(2)}, u32[]{:S(2)}) collective-permute-start(f32[7,6,1,128]{3,2,1,0:T(1,128)S(1)} %get-tuple-element.215), channel_id=1, source_target_pairs={{1,0},{2,1},{3,2},{4,3},{5,4},{6,5},{7,6},{8,7},{9,8},{10,9},{11,1... | collective-permute-start | bytes 64520 | tf_op jit(solution)/shard_map/ppermute | solution.py:248
  113.6 5.8 %collective-permute-start.15 = (f32[7,6,1,128]{3,2,1,0:T(1,128)S(1)}, f32[7,6,1,128]{3,2,1,0:T(1,128)S(1)}, u32[]{:S(2)}, u32[]{:S(2)}) collective-permute-start(f32[7,6,1,128]{3,2,1,0:T(1,128)S(1)} %get-tuple-element.216), channel_id=1, source_target_pairs={{0,1},{1,2},{2,3},{3,4},{4,5},{5,6},{6,7},{7,8},{8,9},{9,10},{10,1... | collective-permute-start | bytes 64520 | tf_op jit(solution)/shard_map/ppermute | solution.py:247
  119.8 1.2 copy-start.5
  125.3 20.7 %copy-start.8 = (s32[1,8192]{1,0:T(1,128)S(1)}, s32[1,8192]{1,0:T(1,128)}, u32[]{:S(2)}) copy-start(s32[1,8192]{1,0:T(1,128)} %param.17) | copy-start | bytes 98308
  126.6 29.6 %all-to-all-start = ((f32[128,1,192]{2,1,0:T(1,128)}), f32[128,1,192]{2,1,0:T(1,128)S(1)}, u32[]{:S(2)}, u32[]{:S(2)}) async-start(f32[128,1,192]{2,1,0:T(1,128)} %reshape.408), calls=%async_computation | async-start | bytes 262144 | tf_op jit(solution)/shard_map/all_to_all | solution.py:329
  (2 other events, 1.6 us)

commit v2 on v0

v2 whole, which is shorter than its diff:
```python
import functools

import jax
import jax.numpy as jnp
from jax import lax
from jax.experimental import pallas as pl
from jax.experimental.pallas import tpu as pltpu
from jax.sharding import PartitionSpec as P

ITERS = 4
MESH = pl.DeviceIdType.MESH
STEP = 4
GREET = 4
AHEAD = 8
TURNS = [(1, 0), (-1, 0), (1, 1), (1, -1), (-1, 1), (-1, -1), (0, 1), (0, -1)]


def chebyshev_coefficients():
    def add(p, q, scale=1.0):
        size = max(len(p), len(q))
        p, q = (list(p) + [0.0] * (size - len(p)), list(q) + [0.0] * (size - len(q)))
        return [u + scale * v for u, v in zip(p, q)]

    theta, delta = 1.0, 0.75
    sigma = theta / delta
    rho = 1.0 / sigma
    x, r, d = ([0.0], [1.0], [1.0 / theta])
    for _ in range(ITERS):
        image = add(d, [0.0] + [0.125 * v for v in d])
        x = add(x, d)
        r = add(r, image, -1.0)
        rho_new = 1.0 / (2.0 * sigma - rho)
        d = add([rho_new * rho * v for v in d], [2.0 * rho_new / delta * v for v in r])
        rho = rho_new
    return add(x, d)


def lookup(index, rows, row):
    lane = index & 127
    group = index >> 7

    def tree(low, size):
        if size == 1:
            return jnp.take_along_axis(row(low), lane, axis=1, mode="promise_in_bounds")
        size //= 2
        return jnp.where((group & size) != 0, tree(low + size, size), tree(low, size))

    return tree(0, rows)


def gather_pair(fields, source, weight, pair, store):
    at = pl.ds(pl.multiple_of(8 * pair, 8), 8)
    index = source[at, :]
    wgt = weight[at, :]
    for f in range(7):

        def row(r):
            return jnp.broadcast_to(fields[f : f + 1, 128 * r : 128 * r + 128], (8, 128))

        store(f, lookup(index, 32, row) * wgt)


def scatter_pairs(arrived, target, total, pairs):
    iota = lax.broadcasted_iota(jnp.int32, (16, 128), 0).astype(jnp.int16)
    one = jnp.ones((16, 128), jnp.bfloat16)
    zero = jnp.zeros((16, 128), jnp.bfloat16)
    columns, values = [], []
    for slot, pair in pairs:
        for row in range(8):
            half, r = divmod(row, 4)
            cell = jnp.broadcast_to(target[pl.ds(8 * pair + row, 1), :], (16, 128))
            x = cell >> 11
            col = (((x & 1) << 7) + (cell & 127)).astype(jnp.int16)
            up = (((x >> 1) << 4) + ((cell >> 7) & 15)).astype(jnp.int16)
            columns.append(
                jnp.concatenate(
                    [jnp.where(iota == col - jnp.int16(16 * i), one, zero) for i in range(16)], axis=0
                )
            )
            here = [iota == up - jnp.int16(16 * i) for i in range(2)]
            high, low = [], []
            for f in range(7):
                val = jnp.broadcast_to(arrived[2 * slot + half, f, r : r + 1, :], (16, 128))
                top = val.astype(jnp.bfloat16)
                rest = (val - top.astype(jnp.float32)).astype(jnp.bfloat16)
                high += [jnp.where(m, top, zero) for m in here]
                low += [jnp.where(m, rest, zero) for m in here]
            values.append(jnp.concatenate(high + low, axis=0))
    total[...] += lax.dot_general(
        jnp.concatenate(values, axis=1),
        jnp.concatenate(columns, axis=1),
        (((1,), (1,)), ((), ())),
        preferred_element_type=jnp.float32,
    )


def cell_moduli(vals):
    phi = vals[0]
    mean = (vals[1] + vals[2] + vals[3]) / 3.0
    q2 = 1.5 * (
        (vals[1] - mean) ** 2
        + (vals[2] - mean) ** 2
        + (vals[3] - mean) ** 2
        + 2.0 * (vals[4] ** 2 + vals[5] ** 2 + vals[6] ** 2)
    )
    bulk = 1.6 * jnp.exp(-3.0 * phi) * (1.0 + 0.25 * jnp.tanh(mean))
    shear = 0.9 * jnp.exp(-2.0 * phi) / (1.0 + q2 / 0.5)
    soften = shear * q2 / (0.5 + q2)
    return bulk, shear, soften


def neighbour_sum(before, here, after):
    lane = lax.broadcasted_iota(jnp.int32, here.shape, 1)
    left = jnp.where(lane == 0, 0.0, pltpu.roll(here, 1, 1))
    right = jnp.where(lane == 127, 0.0, pltpu.roll(here, 127, 1))
    rows = here.shape[0]
    return (before + after) + (pltpu.roll(here, 1, 0) + pltpu.roll(here, rows - 1, 0)) + (left + right)


def whole_kernel(
    n_src,
    n_tgt,
    fields_in,
    source_in,
    weight_in,
    target_in,
    mass_in,
    leave_in,
    place_in,
    projected,
    moduli,
    fields,
    source,
    weight,
    target,
    mass,
    leave,
    place,
    outgoing,
    arrived,
    total,
    resid,
    edge,
    beside,
    strips,
    table,
    packed,
    landed,
    load_sem,
    send_sem,
    recv_sem,
    halo_send,
    halo_recv,
    move_send,
    move_recv,
):
    owners = n_src * n_tgt
    pairs = owners // 2
    steps = pairs // STEP
    at_src, at_tgt = lax.axis_index("src"), lax.axis_index("tgt")
    me = at_src * n_tgt + at_tgt
    my_pair, parity = me // 2, me % 2

    loads = [
        pltpu.make_async_copy(a, b, load_sem.at[i])
        for i, (a, b) in enumerate(
            [
                (fields_in, fields),
                (source_in, source),
                (weight_in, weight),
                (target_in, target),
                (mass_in, mass),
                (leave_in, leave),
                (place_in, place),
            ]
        )
    ]
    for load in loads:
        load.start()

    barrier = pltpu.get_barrier_semaphore()

    def greet(k):
        other = (me + k) % owners
        pl.semaphore_signal(
            barrier, inc=1, device_id=(other // n_tgt, other % n_tgt), device_id_type=MESH
        )

    def gather(k):
        for u in range(STEP):
            slot = STEP * k + u

            def store(f, val):
                outgoing[2 * slot, f] = val[:4]
                outgoing[2 * slot + 1, f] = val[4:]

            gather_pair(fields, source, weight, (my_pair + slot) % pairs, store)

    def copy(slot, half, landing):
        other = 2 * ((my_pair + slot) % pairs) + half
        return pltpu.make_async_remote_copy(
            src_ref=outgoing.at[2 * slot + half],
            dst_ref=arrived.at[2 * slot + landing],
            send_sem=send_sem.at[2 * slot + half],
            recv_sem=recv_sem.at[2 * slot + landing],
            device_id=(other // n_tgt, other % n_tgt),
            device_id_type=MESH,
        )

    def each_copy(k, act):
        for u in range(STEP):
            for half in range(2):
                slot = STEP * k + u
                if u == 0:

                    @pl.when((slot > 0) | (parity != half))
                    def _():
                        act(slot, half)

                else:
                    act(slot, half)

    def launch(k):
        each_copy(k, lambda slot, half: copy(slot, half, parity).start())

    def take(k):
        each_copy(k, lambda slot, half: copy(slot, half, half).wait_recv())

    def scatter(k):
        scatter_pairs(
            arrived,
            target,
            total,
            [(STEP * k + u, (my_pair - STEP * k - u + pairs) % pairs) for u in range(STEP)],
        )

    def greet_all(k, carry):
        greet(k)
        return carry

    lax.fori_loop(1, owners, greet_all, 0)
    total[...] = jnp.zeros_like(total)

    @pl.when(at_src == 0)
    def _():
        beside[0] = jnp.zeros_like(beside[0])
        strips[0] = jnp.zeros_like(strips[0])

    @pl.when(at_src == n_src - 1)
    def _():
        beside[1] = jnp.zeros_like(beside[1])
        strips[2] = jnp.zeros_like(strips[2])

    for side, end in ((0, n_tgt - 1), (1, 0)):

        @pl.when(at_tgt == end)
        def _():
            for block in range(3):
                strips[block, side] = jnp.zeros_like(strips[block, side])

    for load in loads:
        load.wait()

    def gather_only(k, carry):
        gather(k)
        return carry

    def launch_only(k, carry):
        launch(k)
        return carry

    def gather_launch(k, carry):
        gather(k)
        launch(k)
        return carry

    def gather_scatter(k, carry):
        take(k)
        gather(k + AHEAD)
        scatter(k)
        launch(k + AHEAD)
        return carry

    def scatter_only(k, carry):
        take(k)
        scatter(k)
        return carry

    lax.fori_loop(0, GREET, gather_only, 0)
    pl.semaphore_wait(barrier, owners - 1)
    lax.fori_loop(0, GREET, launch_only, 0)
    arrived[parity] = outgoing[parity]
    lax.fori_loop(GREET, AHEAD, gather_launch, 0)
    lax.fori_loop(0, steps - AHEAD, gather_scatter, 0)
    lax.fori_loop(steps - AHEAD, steps, scatter_only, 0)

    inverse = [lax.rsqrt(mass[x]) for x in range(4)]
    for f in range(7):
        for x in range(4):
            rows = pl.ds(32 * f + 16 * (x // 2), 16)
            lower = pl.ds(224 + 32 * f + 16 * (x // 2), 16)
            cols = pl.ds(128 * (x % 2), 128)
            val = (total[rows, cols] + total[lower, cols]) * inverse[x]
            resid[f, x] = val
            edge[0, f, x] = val[:4]
            edge[1, f, x] = val[12:]

    def halo(i):
        da, db = TURNS[i]
        if db == 0:
            src, dst = resid, beside.at[0 if da == 1 else 1]
        else:
            side = 1 if db == 1 else 0
            src, dst = edge.at[side], strips.at[1 - da, side]
        return pltpu.make_async_remote_copy(
            src_ref=src,
            dst_ref=dst,
            send_sem=halo_send.at[i],
            recv_sem=halo_recv.at[i],
            device_id=((at_src + da + n_src) % n_src, (at_tgt + db + n_tgt) % n_tgt),
            device_id_type=MESH,
        )

    def inside(i, sign):
        da, db = TURNS[i]
        a, b = at_src + sign * da, at_tgt + sign * db
        return (a >= 0) & (a < n_src) & (b >= 0) & (b < n_tgt)

    for i in range(8):

        @pl.when(inside(i, 1))
        def _():
            halo(i).start()

    for i in range(8):

        @pl.when(inside(i, -1))
        def _():
            halo(i).wait_recv()

    coefs = chebyshev_coefficients()
    row_id = lax.broadcasted_iota(jnp.int32, (24, 128), 0)
    has_next = (at_tgt < n_tgt - 1).astype(jnp.float32)
    has_last = (at_tgt > 0).astype(jnp.float32)
    valid = jnp.where(row_id < 16, 1.0, jnp.where(row_id < 20, has_next, has_last))
    valid_of = [
        valid * (at_src > 0).astype(jnp.float32),
        valid,
        valid * (at_src < n_src - 1).astype(jnp.float32),
    ]

    def sweeps(f, carry):
        planes = []
        for p in range(12):
            block, q = divmod(p, 4)
            main = resid[f, q] if block == 1 else beside[block // 2, f, q]
            planes.append(jnp.concatenate([main, strips[block, 0, f, q], strips[block, 1, f, q]], axis=0))
        state = [coefs[ITERS] * v for v in planes]
        for depth in range(1, ITERS + 1):
            fresh = list(state)
            for p in range(depth, 12 - depth):
                val = neighbour_sum(state[p - 1], state[p], state[p + 1]) + coefs[ITERS - depth] * planes[p]
                fresh[p] = val if depth == ITERS else val * valid_of[p // 4]
            state = fresh
        for x in range(4):
            projected[f, x] = state[4 + x][:16] * inverse[x]
        return carry

    lax.fori_loop(0, 7, sweeps, 0)

    for x in range(4):
        for h in range(2):
            got = cell_moduli([projected[f, x, 8 * h : 8 * h + 8, :] for f in range(7)])
            for m in range(3):
                table[m, 16 * x + 8 * h : 16 * x + 8 * h + 8, :] = got[m]

    lower_half = lax.broadcasted_iota(jnp.int32, (8, 128), 1) < 64

    def swapped(v):
        return pltpu.roll(v, 64, 1)

    def move(sender, other):
        return pltpu.make_async_remote_copy(
            src_ref=packed.at[other],
            dst_ref=landed.at[sender],
            send_sem=move_send.at[other],
            recv_sem=move_recv.at[sender],
            device_id=(other // n_tgt, other % n_tgt),
            device_id_type=MESH,
        )

    def send_group(step, carry):
        group = (step + my_pair // 8) % 8
        index = leave[pl.ds(pl.multiple_of(8 * group, 8), 8), :]
        bulk, shear, soften = [
            lookup(index, 64, lambda r: jnp.broadcast_to(table[m, r : r + 1, :], (8, 128)))
            for m in range(3)
        ]
        even = jnp.full((8, 128), parity, jnp.int32) == 0
        one = jnp.where(even, bulk, shear)
        two = jnp.where(even, shear, bulk)
        soft_swapped = swapped(soften)
        blocks = [
            [jnp.where(lower_half, one, swapped(two)), jnp.where(even, soften, soft_swapped)],
            [jnp.where(lower_half, swapped(one), two), jnp.where(even, soft_swapped, soften)],
        ]
        for i in range(8):
            for half in range(2):
                other = 16 * group + 2 * i + half
                for r in range(2):
                    packed[other, r : r + 1, :] = blocks[half][r][i : i + 1, :]
        for i in range(16):
            other = 16 * group + i

            @pl.when(other != me)
            def _():
                move(me, other).start()

        return carry

    lax.fori_loop(0, 8, send_group, 0)
    landed[me] = packed[me]

    def receive(k, carry):
        sender = (me + k) % owners
        move(sender, sender).wait_recv()
        return carry

    lax.fori_loop(1, owners, receive, 0)

    def fill(step, carry):
        index = place[pl.ds(pl.multiple_of(8 * step, 8), 8), :]

        def row(m, r):
            first, second = [
                jnp.broadcast_to(landed[2 * r + i, m // 2 : m // 2 + 1, :], (8, 128)) for i in range(2)
            ]
            return jnp.where(lower_half, second, first) if m == 1 else jnp.where(lower_half, first, second)

        for m in range(3):
            at = index ^ 64 if m == 1 else index
            moduli[m, pl.ds(pl.multiple_of(8 * step, 8), 8), :] = lookup(at, 64, functools.partial(row, m))
        return carry

    lax.fori_loop(0, 8, fill, 0)

    def drain(k, carry):
        move((me + k) % owners, (me + k) % owners).wait_send()
        return carry

    def drain_copies(k, carry):
        each_copy(k, lambda slot, half: copy(slot, half, half).wait_send())
        return carry

    lax.fori_loop(0, steps, drain_copies, 0)
    lax.fori_loop(1, owners, drain, 0)
    for i in range(8):

        @pl.when(inside(i, 1))
        def _():
            halo(i).wait_send()


def on_device(
    source_fields, slot_source, slot_weight, slot_target, cell_mass, send_order, place_order
):
    n_src = lax.axis_size("src")
    n_tgt = lax.axis_size("tgt")
    owners = n_src * n_tgt
    hx, hy, hz = cell_mass.shape
    cells = hx * hy * hz
    f32, i32 = jnp.float32, jnp.int32
    args = (
        source_fields,
        slot_source.reshape(4 * owners, 128),
        slot_weight.reshape(4 * owners, 128),
        slot_target.reshape(4 * owners, 128),
        cell_mass,
        send_order.reshape(cells // 128, 128),
        place_order.reshape(cells // 128, 128),
    )
    vmem = pl.BlockSpec(memory_space=pltpu.VMEM)
    projected, moduli = pl.pallas_call(
        functools.partial(whole_kernel, n_src, n_tgt),
        out_shape=(
            jax.ShapeDtypeStruct((7, hx, hy, hz), f32),
            jax.ShapeDtypeStruct((3, cells // 128, 128), f32),
        ),
        in_specs=[pl.BlockSpec(memory_space=pltpu.HBM)] * len(args),
        out_specs=(vmem, vmem),
        scratch_shapes=[pltpu.VMEM(a.shape, a.dtype) for a in args]
        + [
            pltpu.VMEM((owners, 7, 4, 128), f32),
            pltpu.VMEM((owners, 7, 4, 128), f32),
            pltpu.VMEM((448, 256), f32),
            pltpu.VMEM((7, hx, hy, hz), f32),
            pltpu.VMEM((2, 7, hx, 4, hz), f32),
            pltpu.VMEM((2, 7, hx, hy, hz), f32),
            pltpu.VMEM((3, 2, 7, hx, 4, hz), f32),
            pltpu.VMEM((3, cells // 128, 128), f32),
            pltpu.VMEM((owners, 2, 128), f32),
            pltpu.VMEM((owners, 2, 128), f32),
            pltpu.SemaphoreType.DMA((len(args),)),
            pltpu.SemaphoreType.DMA((owners,)),
            pltpu.SemaphoreType.DMA((owners,)),
            pltpu.SemaphoreType.DMA((8,)),
            pltpu.SemaphoreType.DMA((8,)),
            pltpu.SemaphoreType.DMA((owners,)),
            pltpu.SemaphoreType.DMA((owners,)),
        ],
        compiler_params=pltpu.CompilerParams(
            collective_id=0, has_side_effects=True, vmem_limit_bytes=60 << 20
        ),
    )(*args)
    return projected, moduli.reshape(3, cells)


def solution(mesh):
    placed = (
        P(None, ("src", "tgt")),
        P(("src", "tgt")),
        P(("src", "tgt")),
        P(("src", "tgt")),
        P("src", "tgt", None),
        P(("src", "tgt"), None),
        P(("src", "tgt"), None),
    )
    return jax.shard_map(
        on_device,
        mesh=mesh,
        in_specs=placed,
        out_specs=(P(None, "src", "tgt", None), P(None, ("src", "tgt"))),
        check_vma=False,
    )
```

time: 309 us -> 78.3 us (0.25)
  matrix products: 105 us -> 0 us
  starting transfers between devices: 78.8 us -> 0 us
  Pallas kernels: 0 us -> 75.1 us
  other arithmetic: 53.5 us -> 0 us
  waiting for transfers between devices: 46.2 us -> 0 us
  local copies, waits for them, and re-layouts: 21.1 us -> 2.35 us
    dot_general x36 -> x0, matrix products: 105 us -> none  [the longest x16 72.1 us: add_block(): lax.dot_general(onehot, spread, (((0,), (0,)), ((), ())), precision=lax.P...]
    pallas_call x0 -> x1, Pallas kernels: none -> 75.1 us  [on_device(): pl.pallas_call(functools.partial(whole_kernel, n_src, n_tgt), out_shape=(...]
    ppermute x16 -> x0, starting transfers between devices: 50.3 us -> none  [the longest x8 35 us: padded_2(): before = lax.ppermute(last, axis, up)]
    all_to_all x2 -> x0, waiting for transfers between devices: 38.6 us -> none  [the longest x1 29.1 us: on_device(): lax.all_to_all(values, ('src', 'tgt'), split_axis=1, concat_axis=1, tiled...]
    mul x22 -> x0, other arithmetic: 36.2 us -> none  [the longest x16 35.2 us: add_block(): spread = (vals.T[:, :, None] * lanes[:, None, :]).reshape(block, rows * 32)]
    all_to_all x2 -> x0, starting transfers between devices: 28.6 us -> none  [the longest x1 17.1 us: on_device(): lax.all_to_all(outgoing.reshape(rows, owners, quota), ('src', 'tgt'), spl...]
    reduce_sum x20 -> x0, other arithmetic: 9.92 us -> none  [one_block(): return jnp.sum(picked * lanes[None], axis=1)]
    ppermute x16 -> x0, waiting for transfers between devices: 7.58 us -> none  [the longest x8 7.56 us: padded_2(): before = lax.ppermute(last, axis, up)]
  transfers between devices with their start and end apart: 18 -> 0, of which waited for: 9 -> 0; matrix products, arithmetic and copies ran while one was open for 1% -> 0% of each run, Pallas kernels for 0% -> 0%
where the time goes in v2:
time: 78.3 us; the launch traced here: 78.1 us
  Pallas kernels  75.1 us (96%)
  local copies, waits for them, and re-layouts  2.35 us (3%)
    pallas_call x1, Pallas kernels, on_device(): pl.pallas_call(functools.partial(whole_kernel, n_src, n_tgt), out_shape=(...  75.1 us
    unnamed x4, local copies, waits for them, and re-layouts  2.35 us

profile of v2, /device:TPU:1, one launch (start us, length us, event | category | flops | bytes accessed | tf_op | source)
XLA Modules:
  0.0 78.1 jit_solution(16556335426356989936)
XLA Ops:
  0.6 75.1 %shard_map.86 = (f32[7,4,16,128]{3,2,1,0:T(8,128)}, f32[3,64,128]{2,1,0:T(8,128)}) custom-call(f32[7,4096]{1,0:T(8,128)} %fields_in.1, s32[512,128]{1,0:T(8,128)} %bitcast.9, f32[512,128]{1,0:T(8,128)} %bitcast.10, s32[512,128]{1,0:T(8,128)} %bitcast.11, f32[4,16,128]{2,1,0:T(8,128)} %mass_in.1, s32[64,128]{1,0:T(8,128)} %bitcast.14, s32[64,128]{1,0:T(8,128)} %bitcast.15), custom_call_target="tpu_custom_call" | custom-call | tf_op jit(solution)/shard_map/pallas_call | solution.py:483
  75.8 0.0 copy-start
  75.8 1.7 %copy.11 = f32[1,3,64,128]{3,1,2,0:T(4,128)} copy(f32[1,3,64,128]{3,2,1,0:T(8,128)} %bitcast.13) | data formatting | bytes 196608
  77.4 0.0 copy-done
  77.5 0.7 copy.13
Async XLA Ops:
  75.8 1.7 %copy-start = (f32[7,4,16,128]{3,2,1,0:T(8,128)S(1)}, f32[7,4,16,128]{3,2,1,0:T(8,128)}, u32[]{:S(2)}) copy-start(f32[7,4,16,128]{3,2,1,0:T(8,128)} %get-tuple-element.8) | copy-start | bytes 688132

commit v3 on v2

--- a/solution.py
+++ b/solution.py
@@ -145,14 +145,17 @@
     strips,
     table,
     packed,
+    midway,
     landed,
     load_sem,
     send_sem,
     recv_sem,
     halo_send,
     halo_recv,
-    move_send,
-    move_recv,
+    across_send,
+    across_recv,
+    along_send,
+    along_recv,
 ):
     owners = n_src * n_tgt
     pairs = owners // 2
@@ -180,12 +183,6 @@
 
     barrier = pltpu.get_barrier_semaphore()
 
-    def greet(k):
-        other = (me + k) % owners
-        pl.semaphore_signal(
-            barrier, inc=1, device_id=(other // n_tgt, other % n_tgt), device_id_type=MESH
-        )
-
     def gather(k):
         for u in range(STEP):
             slot = STEP * k + u
@@ -234,11 +231,19 @@
             [(STEP * k + u, (my_pair - STEP * k - u + pairs) % pairs) for u in range(STEP)],
         )
 
-    def greet_all(k, carry):
-        greet(k)
-        return carry
-
-    lax.fori_loop(1, owners, greet_all, 0)
+    def greet_row(k, carry):
+        row = lax.rem(at_src + k, n_src)
+        for j in range(n_tgt):
+            pl.semaphore_signal(
+                barrier, inc=1, device_id=(row, lax.rem(at_tgt + j, n_tgt)), device_id_type=MESH
+            )
+        return carry
+
+    for j in range(1, n_tgt):
+        pl.semaphore_signal(
+            barrier, inc=1, device_id=(at_src, lax.rem(at_tgt + j, n_tgt)), device_id_type=MESH
+        )
+    lax.fori_loop(1, n_src, greet_row, 0)
     total[...] = jnp.zeros_like(total)
 
     @pl.when(at_src == 0)
@@ -379,18 +384,30 @@
     def swapped(v):
         return pltpu.roll(v, 64, 1)
 
-    def move(sender, other):
+    def across(k):
+        other = (at_src + k) % n_src
         return pltpu.make_async_remote_copy(
             src_ref=packed.at[other],
-            dst_ref=landed.at[sender],
-            send_sem=move_send.at[other],
-            recv_sem=move_recv.at[sender],
-            device_id=(other // n_tgt, other % n_tgt),
+            dst_ref=midway.at[at_src],
+            send_sem=across_send.at[k],
+            recv_sem=across_recv.at[k],
+            device_id=(other, at_tgt),
             device_id_type=MESH,
         )
 
+    def along(k):
+        other = (at_tgt + k) % n_tgt
+        return pltpu.make_async_remote_copy(
+            src_ref=midway.at[:, other],
+            dst_ref=landed.at[:, at_tgt],
+            send_sem=along_send.at[k],
+            recv_sem=along_recv.at[k],
+            device_id=(at_src, other),
+            device_id_type=MESH,
+        )
+
     def send_group(step, carry):
-        group = (step + my_pair // 8) % 8
+        group = (step + at_src) % n_src
         index = leave[pl.ds(pl.multiple_of(8 * group, 8), 8), :]
         bulk, shear, soften = [
             lookup(index, 64, lambda r: jnp.broadcast_to(table[m, r : r + 1, :], (8, 128)))
@@ -406,34 +423,32 @@
         ]
         for i in range(8):
             for half in range(2):
-                other = 16 * group + 2 * i + half
                 for r in range(2):
-                    packed[other, r : r + 1, :] = blocks[half][r][i : i + 1, :]
-        for i in range(16):
-            other = 16 * group + i
-
-            @pl.when(other != me)
-            def _():
-                move(me, other).start()
-
-        return carry
-
-    lax.fori_loop(0, 8, send_group, 0)
-    landed[me] = packed[me]
-
-    def receive(k, carry):
-        sender = (me + k) % owners
-        move(sender, sender).wait_recv()
-        return carry
-
-    lax.fori_loop(1, owners, receive, 0)
+                    packed[group, 2 * i + half, r : r + 1, :] = blocks[half][r][i : i + 1, :]
+
+        @pl.when(step < n_src)
+        def _():
+            across(step).start()
+
+        return carry
+
+    lax.fori_loop(1, n_src + 1, send_group, 0)
+    midway[at_src] = packed[at_src]
+    for k in range(1, n_src):
+        across(k).wait_recv()
+    for k in range(1, n_tgt):
+        along(k).start()
+    landed[:, at_tgt] = midway[:, at_tgt]
+    for k in range(1, n_tgt):
+        along(k).wait_recv()
 
     def fill(step, carry):
         index = place[pl.ds(pl.multiple_of(8 * step, 8), 8), :]
 
         def row(m, r):
             first, second = [
-                jnp.broadcast_to(landed[2 * r + i, m // 2 : m // 2 + 1, :], (8, 128)) for i in range(2)
+                jnp.broadcast_to(landed[r // 8, (2 * r + i) % 16, m // 2 : m // 2 + 1, :], (8, 128))
+                for i in range(2)
             ]
             return jnp.where(lower_half, second, first) if m == 1 else jnp.where(lower_half, first, second)
 
@@ -444,16 +459,15 @@
 
     lax.fori_loop(0, 8, fill, 0)
 
-    def drain(k, carry):
-        move((me + k) % owners, (me + k) % owners).wait_send()
-        return carry
-
     def drain_copies(k, carry):
         each_copy(k, lambda slot, half: copy(slot, half, half).wait_send())
         return carry
 
     lax.fori_loop(0, steps, drain_copies, 0)
-    lax.fori_loop(1, owners, drain, 0)
+    for k in range(1, n_src):
+        across(k).wait_send()
+    for k in range(1, n_tgt):
+        along(k).wait_send()
     for i in range(8):
 
         @pl.when(inside(i, 1))
@@ -498,15 +512,18 @@
             pltpu.VMEM((2, 7, hx, hy, hz), f32),
             pltpu.VMEM((3, 2, 7, hx, 4, hz), f32),
             pltpu.VMEM((3, cells // 128, 128), f32),
-            pltpu.VMEM((owners, 2, 128), f32),
-            pltpu.VMEM((owners, 2, 128), f32),
+            pltpu.VMEM((n_src, n_tgt, 2, 128), f32),
+            pltpu.VMEM((n_src, n_tgt, 2, 128), f32),
+            pltpu.VMEM((n_src, n_tgt, 2, 128), f32),
             pltpu.SemaphoreType.DMA((len(args),)),
             pltpu.SemaphoreType.DMA((owners,)),
             pltpu.SemaphoreType.DMA((owners,)),
             pltpu.SemaphoreType.DMA((8,)),
             pltpu.SemaphoreType.DMA((8,)),
-            pltpu.SemaphoreType.DMA((owners,)),
-            pltpu.SemaphoreType.DMA((owners,)),
+            pltpu.SemaphoreType.DMA((n_src,)),
+            pltpu.SemaphoreType.DMA((n_src,)),
+            pltpu.SemaphoreType.DMA((n_tgt,)),
+            pltpu.SemaphoreType.DMA((n_tgt,)),
         ],
         compiler_params=pltpu.CompilerParams(
             collective_id=0, has_side_effects=True, vmem_limit_bytes=60 << 20

time: 78.3 us -> 72.3 us (0.923)
  Pallas kernels: 75.1 us -> 69.2 us
    pallas_call x1, Pallas kernels: 75.1 us -> 69.2 us  [on_device(): pl.pallas_call(functools.partial(whole_kernel, n_src, n_tgt), out_shape=(...]
where the time goes in v3:
time: 72.3 us; the launch traced here: 72.2 us
  Pallas kernels  69.2 us (96%)
  local copies, waits for them, and re-layouts  2.35 us (3%)
    pallas_call x1, Pallas kernels, on_device(): pl.pallas_call(functools.partial(whole_kernel, n_src, n_tgt), out_shape=(...  69.2 us
    unnamed x4, local copies, waits for them, and re-layouts  2.35 us

profile of v3, /device:TPU:1, one launch (start us, length us, event | category | flops | bytes accessed | tf_op | source)
XLA Modules:
  0.0 72.2 jit_solution(6527594216809365802)
XLA Ops:
  0.6 69.2 %shard_map.86 = (f32[7,4,16,128]{3,2,1,0:T(8,128)}, f32[3,64,128]{2,1,0:T(8,128)}) custom-call(f32[7,4096]{1,0:T(8,128)} %fields_in.1, s32[512,128]{1,0:T(8,128)} %bitcast.9, f32[512,128]{1,0:T(8,128)} %bitcast.10, s32[512,128]{1,0:T(8,128)} %bitcast.11, f32[4,16,128]{2,1,0:T(8,128)} %mass_in.1, s32[64,128]{1,0:T(8,128)} %bitcast.14, s32[64,128]{1,0:T(8,128)} %bitcast.15), custom_call_target="tpu_custom_call" | custom-call | tf_op jit(solution)/shard_map/pallas_call | solution.py:497
  69.8 0.0 copy-start
  69.8 1.7 %copy.11 = f32[1,3,64,128]{3,1,2,0:T(4,128)} copy(f32[1,3,64,128]{3,2,1,0:T(8,128)} %bitcast.13) | data formatting | bytes 196608
  71.5 0.0 copy-done
  71.5 0.7 copy.13
Async XLA Ops:
  69.8 1.7 %copy-start = (f32[7,4,16,128]{3,2,1,0:T(8,128)S(1)}, f32[7,4,16,128]{3,2,1,0:T(8,128)}, u32[]{:S(2)}) copy-start(f32[7,4,16,128]{3,2,1,0:T(8,128)} %get-tuple-element.8) | copy-start | bytes 688132

commit v4 on v3

--- a/solution.py
+++ b/solution.py
@@ -10,8 +10,9 @@
 ITERS = 4
 MESH = pl.DeviceIdType.MESH
 STEP = 4
-GREET = 4
-AHEAD = 8
+GREET = 3
+AHEAD = 6
+PARTS = [(0, 2), (2, 2), (4, 3)]
 TURNS = [(1, 0), (-1, 0), (1, 1), (1, -1), (-1, 1), (-1, -1), (0, 1), (0, -1)]
 
 
@@ -126,16 +127,14 @@
     target_in,
     mass_in,
     leave_in,
-    place_in,
     projected,
-    moduli,
+    landed,
     fields,
     source,
     weight,
     target,
     mass,
     leave,
-    place,
     outgoing,
     arrived,
     total,
@@ -146,7 +145,6 @@
     table,
     packed,
     midway,
-    landed,
     load_sem,
     send_sem,
     recv_sem,
@@ -162,7 +160,13 @@
     steps = pairs // STEP
     at_src, at_tgt = lax.axis_index("src"), lax.axis_index("tgt")
     me = at_src * n_tgt + at_tgt
-    my_pair, parity = me // 2, me % 2
+    parity = me % 2
+
+    def pair_at(step, sign):
+        row, col = step % n_src, (step // n_src + step) % (n_tgt // 2)
+        row = (at_src + sign * row + n_src) % n_src
+        col = (at_tgt // 2 + sign * col + n_tgt // 2) % (n_tgt // 2)
+        return row * (n_tgt // 2) + col
 
     loads = [
         pltpu.make_async_copy(a, b, load_sem.at[i])
@@ -174,7 +178,6 @@
                 (target_in, target),
                 (mass_in, mass),
                 (leave_in, leave),
-                (place_in, place),
             ]
         )
     ]
@@ -191,10 +194,10 @@
                 outgoing[2 * slot, f] = val[:4]
                 outgoing[2 * slot + 1, f] = val[4:]
 
-            gather_pair(fields, source, weight, (my_pair + slot) % pairs, store)
+            gather_pair(fields, source, weight, pair_at(slot, 1), store)
 
     def copy(slot, half, landing):
-        other = 2 * ((my_pair + slot) % pairs) + half
+        other = 2 * pair_at(slot, 1) + half
         return pltpu.make_async_remote_copy(
             src_ref=outgoing.at[2 * slot + half],
             dst_ref=arrived.at[2 * slot + landing],
@@ -228,7 +231,7 @@
             arrived,
             target,
             total,
-            [(STEP * k + u, (my_pair - STEP * k - u + pairs) % pairs) for u in range(STEP)],
+            [(STEP * k + u, pair_at(STEP * k + u, -1)) for u in range(STEP)],
         )
 
     def greet_row(k, carry):
@@ -300,28 +303,19 @@
     lax.fori_loop(steps - AHEAD, steps, scatter_only, 0)
 
     inverse = [lax.rsqrt(mass[x]) for x in range(4)]
-    for f in range(7):
-        for x in range(4):
-            rows = pl.ds(32 * f + 16 * (x // 2), 16)
-            lower = pl.ds(224 + 32 * f + 16 * (x // 2), 16)
-            cols = pl.ds(128 * (x % 2), 128)
-            val = (total[rows, cols] + total[lower, cols]) * inverse[x]
-            resid[f, x] = val
-            edge[0, f, x] = val[:4]
-            edge[1, f, x] = val[12:]
-
-    def halo(i):
+    def halo(part, i):
         da, db = TURNS[i]
+        span = pl.ds(*PARTS[part])
         if db == 0:
-            src, dst = resid, beside.at[0 if da == 1 else 1]
+            src, dst = resid.at[span], beside.at[0 if da == 1 else 1, span]
         else:
             side = 1 if db == 1 else 0
-            src, dst = edge.at[side], strips.at[1 - da, side]
+            src, dst = edge.at[side, span], strips.at[1 - da, side, span]
         return pltpu.make_async_remote_copy(
             src_ref=src,
             dst_ref=dst,
-            send_sem=halo_send.at[i],
-            recv_sem=halo_recv.at[i],
+            send_sem=halo_send.at[8 * part + i],
+            recv_sem=halo_recv.at[8 * part + i],
             device_id=((at_src + da + n_src) % n_src, (at_tgt + db + n_tgt) % n_tgt),
             device_id_type=MESH,
         )
@@ -331,18 +325,30 @@
         a, b = at_src + sign * da, at_tgt + sign * db
         return (a >= 0) & (a < n_src) & (b >= 0) & (b < n_tgt)
 
-    for i in range(8):
-
-        @pl.when(inside(i, 1))
-        def _():
-            halo(i).start()
-
-    for i in range(8):
-
-        @pl.when(inside(i, -1))
-        def _():
-            halo(i).wait_recv()
-
+    def each_halo(part, sign, act):
+        for i in range(8):
+
+            @pl.when(inside(i, sign))
+            def _():
+                act(halo(part, i))
+
+    for part, (first, count) in enumerate(PARTS):
+        for f in range(first, first + count):
+            for x in range(4):
+                rows = pl.ds(32 * f + 16 * (x // 2), 16)
+                lower = pl.ds(224 + 32 * f + 16 * (x // 2), 16)
+                cols = pl.ds(128 * (x % 2), 128)
+                val = (total[rows, cols] + total[lower, cols]) * inverse[x]
+                resid[f, x] = val
+                edge[0, f, x] = val[:4]
+                edge[1, f, x] = val[12:]
+        each_halo(part, 1, lambda sent: sent.start())
+
+    def drain_copies(k, carry):
+        each_copy(k, lambda slot, half: copy(slot, half, half).wait_send())
+        return carry
+
+    lax.fori_loop(0, steps, drain_copies, 0)
     coefs = chebyshev_coefficients()
     row_id = lax.broadcasted_iota(jnp.int32, (24, 128), 0)
     has_next = (at_tgt < n_tgt - 1).astype(jnp.float32)
@@ -371,7 +377,9 @@
             projected[f, x] = state[4 + x][:16] * inverse[x]
         return carry
 
-    lax.fori_loop(0, 7, sweeps, 0)
+    for part, (first, count) in enumerate(PARTS):
+        each_halo(part, -1, lambda came: came.wait_recv())
+        lax.fori_loop(first, first + count, sweeps, 0)
 
     for x in range(4):
         for h in range(2):
@@ -442,6 +450,18 @@
     for k in range(1, n_tgt):
         along(k).wait_recv()
 
+    for k in range(1, n_src):
+        across(k).wait_send()
+    for k in range(1, n_tgt):
+        along(k).wait_send()
+    for part in range(len(PARTS)):
+        each_halo(part, 1, lambda sent: sent.wait_send())
+
+
+def place_kernel(landed, place, projected_in, projected, moduli):
+    projected[...] = projected_in[...]
+    lower_half = lax.broadcasted_iota(jnp.int32, (8, 128), 1) < 64
+
     def fill(step, carry):
         index = place[pl.ds(pl.multiple_of(8 * step, 8), 8), :]
 
@@ -454,25 +474,12 @@
 
         for m in range(3):
             at = index ^ 64 if m == 1 else index
-            moduli[m, pl.ds(pl.multiple_of(8 * step, 8), 8), :] = lookup(at, 64, functools.partial(row, m))
+            got = lookup(at, 64, functools.partial(row, m))
+            for i in range(8):
+                moduli[m : m + 1, pl.ds(pl.multiple_of(1024 * step + 128 * i, 128), 128)] = got[i : i + 1]
         return carry
 
     lax.fori_loop(0, 8, fill, 0)
-
-    def drain_copies(k, carry):
-        each_copy(k, lambda slot, half: copy(slot, half, half).wait_send())
-        return carry
-
-    lax.fori_loop(0, steps, drain_copies, 0)
-    for k in range(1, n_src):
-        across(k).wait_send()
-    for k in range(1, n_tgt):
-        along(k).wait_send()
-    for i in range(8):
-
-        @pl.when(inside(i, 1))
-        def _():
-            halo(i).wait_send()
 
 
 def on_device(
@@ -491,14 +498,13 @@
         slot_target.reshape(4 * owners, 128),
         cell_mass,
         send_order.reshape(cells // 128, 128),
-        place_order.reshape(cells // 128, 128),
     )
     vmem = pl.BlockSpec(memory_space=pltpu.VMEM)
-    projected, moduli = pl.pallas_call(
+    computed, landed = pl.pallas_call(
         functools.partial(whole_kernel, n_src, n_tgt),
         out_shape=(
             jax.ShapeDtypeStruct((7, hx, hy, hz), f32),
-            jax.ShapeDtypeStruct((3, cells // 128, 128), f32),
+            jax.ShapeDtypeStruct((n_src, n_tgt, 2, 128), f32),
         ),
         in_specs=[pl.BlockSpec(memory_space=pltpu.HBM)] * len(args),
         out_specs=(vmem, vmem),
@@ -514,12 +520,11 @@
             pltpu.VMEM((3, cells // 128, 128), f32),
             pltpu.VMEM((n_src, n_tgt, 2, 128), f32),
             pltpu.VMEM((n_src, n_tgt, 2, 128), f32),
-            pltpu.VMEM((n_src, n_tgt, 2, 128), f32),
             pltpu.SemaphoreType.DMA((len(args),)),
             pltpu.SemaphoreType.DMA((owners,)),
             pltpu.SemaphoreType.DMA((owners,)),
-            pltpu.SemaphoreType.DMA((8,)),
-            pltpu.SemaphoreType.DMA((8,)),
+            pltpu.SemaphoreType.DMA((8 * len(PARTS),)),
+            pltpu.SemaphoreType.DMA((8 * len(PARTS),)),
             pltpu.SemaphoreType.DMA((n_src,)),
             pltpu.SemaphoreType.DMA((n_src,)),
             pltpu.SemaphoreType.DMA((n_tgt,)),
@@ -529,7 +534,15 @@
             collective_id=0, has_side_effects=True, vmem_limit_bytes=60 << 20
         ),
     )(*args)
-    return projected, moduli.reshape(3, cells)
+    return pl.pallas_call(
+        place_kernel,
+        out_shape=(
+            jax.ShapeDtypeStruct((7, hx, hy, hz), f32),
+            jax.ShapeDtypeStruct((3, cells), f32),
+        ),
+        in_specs=(vmem, vmem, vmem),
+        out_specs=(vmem, vmem),
+    )(landed, place_order.reshape(cells // 128, 128), computed)
 
 
 def solution(mesh):

time: 72.3 us -> 65.7 us (0.909)
  Pallas kernels: 69.2 us -> 65 us
  local copies, waits for them, and re-layouts: 2.35 us -> 0 us
    pallas_call x1, Pallas kernels: 69.2 us -> 61 us  [on_device(): pl.pallas_call(functools.partial(whole_kernel, n_src, n_tgt), out_shape=(...]
    pallas_call x0 -> x1, Pallas kernels: none -> 4 us  [on_device(): pl.pallas_call(place_kernel, out_shape=(jax.ShapeDtypeStruct((7, hx, hy,...]
    unnamed x4 -> x0, local copies, waits for them, and re-layouts: 2.35 us -> none
where the time goes in v4:
time: 65.7 us; the launch traced here: 65.6 us
  Pallas kernels  65 us (99%)
    pallas_call x1, Pallas kernels, on_device(): pl.pallas_call(functools.partial(whole_kernel, n_src, n_tgt), out_shape=(...  61 us
    pallas_call x1, Pallas kernels, on_device(): pl.pallas_call(place_kernel, out_shape=(jax.ShapeDtypeStruct((7, hx, hy,...  4 us

profile of v4, /device:TPU:1, one launch (start us, length us, event | category | flops | bytes accessed | tf_op | source)
XLA Modules:
  0.0 65.6 jit_solution(14734667741114302645)
XLA Ops:
  0.6 61.0 %shard_map.86 = (f32[7,4,16,128]{3,2,1,0:T(8,128)}, f32[8,16,2,128]{3,2,1,0:T(2,128)}) custom-call(f32[7,4096]{1,0:T(8,128)} %fields_in.1, s32[512,128]{1,0:T(8,128)} %bitcast.5, f32[512,128]{1,0:T(8,128)} %bitcast.6, s32[512,128]{1,0:T(8,128)} %bitcast.7, f32[4,16,128]{2,1,0:T(8,128)} %mass_in.1, s32[64,128]{1,0:T(8,128)} %bitcast.8), custom_call_target="tpu_custom_call" | custom-call | tf_op jit(solution)/shard_map/pallas_call | solution.py:503
  61.6 4.0 %shard_map.87 = (f32[7,4,16,128]{3,2,1,0:T(8,128)}, f32[3,8192]{1,0:T(4,128)}) custom-call(f32[8,16,2,128]{3,2,1,0:T(2,128)} %get-tuple-element.4.landed, s32[64,128]{1,0:T(8,128)} %bitcast.9, f32[7,4,16,128]{3,2,1,0:T(8,128)} %get-tuple-element.5.projected_in), custom_call_target="tpu_custom_call" | custom-call | tf_op jit(solution)/shard_map/pallas_call | solution.py:537

commit v5 on v4

--- a/solution.py
+++ b/solution.py
@@ -127,7 +127,7 @@
     target_in,
     mass_in,
     leave_in,
-    projected,
+    computed,
     landed,
     fields,
     source,
@@ -145,6 +145,7 @@
     table,
     packed,
     midway,
+    projected,
     load_sem,
     send_sem,
     recv_sem,
@@ -154,6 +155,7 @@
     across_recv,
     along_send,
     along_recv,
+    keep_sem,
 ):
     owners = n_src * n_tgt
     pairs = owners // 2
@@ -235,18 +237,18 @@
         )
 
     def greet_row(k, carry):
-        row = lax.rem(at_src + k, n_src)
+        row = lax.rem(at_src + lax.rem(k + n_src // 2 - 2, n_src - 1) + 1, n_src)
         for j in range(n_tgt):
             pl.semaphore_signal(
                 barrier, inc=1, device_id=(row, lax.rem(at_tgt + j, n_tgt)), device_id_type=MESH
             )
         return carry
 
+    lax.fori_loop(1, n_src, greet_row, 0)
     for j in range(1, n_tgt):
         pl.semaphore_signal(
             barrier, inc=1, device_id=(at_src, lax.rem(at_tgt + j, n_tgt)), device_id_type=MESH
         )
-    lax.fori_loop(1, n_src, greet_row, 0)
     total[...] = jnp.zeros_like(total)
 
     @pl.when(at_src == 0)
@@ -380,6 +382,9 @@
     for part, (first, count) in enumerate(PARTS):
         each_halo(part, -1, lambda came: came.wait_recv())
         lax.fori_loop(first, first + count, sweeps, 0)
+
+    keep = pltpu.make_async_copy(projected, computed, keep_sem)
+    keep.start()
 
     for x in range(4):
         for h in range(2):
@@ -454,12 +459,15 @@
         across(k).wait_send()
     for k in range(1, n_tgt):
         along(k).wait_send()
+    keep.wait()
     for part in range(len(PARTS)):
         each_halo(part, 1, lambda sent: sent.wait_send())
 
 
-def place_kernel(landed, place, projected_in, projected, moduli):
-    projected[...] = projected_in[...]
+def place_kernel(landed, place, computed, projected, moduli, passing, sem):
+    bring = pltpu.make_async_copy(computed, passing, sem.at[0])
+    keep = pltpu.make_async_copy(passing, projected, sem.at[1])
+    bring.start()
     lower_half = lax.broadcasted_iota(jnp.int32, (8, 128), 1) < 64
 
     def fill(step, carry):
@@ -479,7 +487,11 @@
                 moduli[m : m + 1, pl.ds(pl.multiple_of(1024 * step + 128 * i, 128), 128)] = got[i : i + 1]
         return carry
 
-    lax.fori_loop(0, 8, fill, 0)
+    lax.fori_loop(0, 4, fill, 0)
+    bring.wait()
+    keep.start()
+    lax.fori_loop(4, 8, fill, 0)
+    keep.wait()
 
 
 def on_device(
@@ -500,6 +512,7 @@
         send_order.reshape(cells // 128, 128),
     )
     vmem = pl.BlockSpec(memory_space=pltpu.VMEM)
+    far = pl.BlockSpec(memory_space=pl.ANY)
     computed, landed = pl.pallas_call(
         functools.partial(whole_kernel, n_src, n_tgt),
         out_shape=(
@@ -507,7 +520,7 @@
             jax.ShapeDtypeStruct((n_src, n_tgt, 2, 128), f32),
         ),
         in_specs=[pl.BlockSpec(memory_space=pltpu.HBM)] * len(args),
-        out_specs=(vmem, vmem),
+        out_specs=(far, vmem),
         scratch_shapes=[pltpu.VMEM(a.shape, a.dtype) for a in args]
         + [
             pltpu.VMEM((owners, 7, 4, 128), f32),
@@ -520,6 +533,7 @@
             pltpu.VMEM((3, cells // 128, 128), f32),
             pltpu.VMEM((n_src, n_tgt, 2, 128), f32),
             pltpu.VMEM((n_src, n_tgt, 2, 128), f32),
+            pltpu.VMEM((7, hx, hy, hz), f32),
             pltpu.SemaphoreType.DMA((len(args),)),
             pltpu.SemaphoreType.DMA((owners,)),
             pltpu.SemaphoreType.DMA((owners,)),
@@ -529,6 +543,7 @@
             pltpu.SemaphoreType.DMA((n_src,)),
             pltpu.SemaphoreType.DMA((n_tgt,)),
             pltpu.SemaphoreType.DMA((n_tgt,)),
+            pltpu.SemaphoreType.DMA,
         ],
         compiler_params=pltpu.CompilerParams(
             collective_id=0, has_side_effects=True, vmem_limit_bytes=60 << 20
@@ -540,8 +555,9 @@
             jax.ShapeDtypeStruct((7, hx, hy, hz), f32),
             jax.ShapeDtypeStruct((3, cells), f32),
         ),
-        in_specs=(vmem, vmem, vmem),
-        out_specs=(vmem, vmem),
+        in_specs=(vmem, vmem, far),
+        out_specs=(far, vmem),
+        scratch_shapes=[pltpu.VMEM((7, hx, hy, hz), f32), pltpu.SemaphoreType.DMA((2,))],
     )(landed, place_order.reshape(cells // 128, 128), computed)
 
 

time: 65.7 us -> 65.3 us (level)
  no operation moved by 1% of the time
where the time goes in v5:
time: 65.3 us; the launch traced here: 65.2 us
  Pallas kernels  64.6 us (99%)
    pallas_call x1, Pallas kernels, on_device(): pl.pallas_call(functools.partial(whole_kernel, n_src, n_tgt), out_shape=(...  60.7 us
    pallas_call x1, Pallas kernels, on_device(): pl.pallas_call(place_kernel, out_shape=(jax.ShapeDtypeStruct((7, hx, hy,...  3.89 us

profile of v5, /device:TPU:1, one launch (start us, length us, event | category | flops | bytes accessed | tf_op | source)
XLA Modules:
  0.0 65.2 jit_solution(6711757597979978652)
XLA Ops:
  0.6 60.7 %shard_map.86 = (f32[7,4,16,128]{3,2,1,0:T(8,128)}, f32[8,16,2,128]{3,2,1,0:T(2,128)}) custom-call(f32[7,4096]{1,0:T(8,128)} %fields_in.1, s32[512,128]{1,0:T(8,128)} %bitcast.5, f32[512,128]{1,0:T(8,128)} %bitcast.6, s32[512,128]{1,0:T(8,128)} %bitcast.7, f32[4,16,128]{2,1,0:T(8,128)} %mass_in.1, s32[64,128]{1,0:T(8,128)} %bitcast.8), custom_call_target="tpu_custom_call" | custom-call | tf_op jit(solution)/shard_map/pallas_call | solution.py:516
  61.3 3.9 %shard_map.87 = (f32[7,4,16,128]{3,2,1,0:T(8,128)}, f32[3,8192]{1,0:T(4,128)}) custom-call(f32[8,16,2,128]{3,2,1,0:T(2,128)} %get-tuple-element.4.landed, s32[64,128]{1,0:T(8,128)} %bitcast.9, f32[7,4,16,128]{3,2,1,0:T(8,128)} %get-tuple-element.5.computed), custom_call_target="tpu_custom_call" | custom-call | tf_op jit(solution)/shard_map/pallas_call | solution.py:552

commit v6 on v5

--- a/solution.py
+++ b/solution.py
@@ -10,9 +10,9 @@
 ITERS = 4
 MESH = pl.DeviceIdType.MESH
 STEP = 4
-GREET = 3
+GREET = 2
 AHEAD = 6
-PARTS = [(0, 2), (2, 2), (4, 3)]
+PARTS = [(0, 1), (1, 2), (3, 2), (5, 2)]
 TURNS = [(1, 0), (-1, 0), (1, 1), (1, -1), (-1, 1), (-1, -1), (0, 1), (0, -1)]
 
 

time: 65.3 us -> 65.3 us (level)
  no operation moved by 1% of the time
where the time goes in v6:
time: 65.3 us; the launch traced here: 65.1 us
  Pallas kernels  64.5 us (99%)
    pallas_call x1, Pallas kernels, on_device(): pl.pallas_call(functools.partial(whole_kernel, n_src, n_tgt), out_shape=(...  60.6 us
    pallas_call x1, Pallas kernels, on_device(): pl.pallas_call(place_kernel, out_shape=(jax.ShapeDtypeStruct((7, hx, hy,...  3.89 us

profile of v6, /device:TPU:1, one launch (start us, length us, event | category | flops | bytes accessed | tf_op | source)
XLA Modules:
  0.0 65.1 jit_solution(1951510558142456284)
XLA Ops:
  0.6 60.6 %shard_map.86 = (f32[7,4,16,128]{3,2,1,0:T(8,128)}, f32[8,16,2,128]{3,2,1,0:T(2,128)}) custom-call(f32[7,4096]{1,0:T(8,128)} %fields_in.1, s32[512,128]{1,0:T(8,128)} %bitcast.5, f32[512,128]{1,0:T(8,128)} %bitcast.6, s32[512,128]{1,0:T(8,128)} %bitcast.7, f32[4,16,128]{2,1,0:T(8,128)} %mass_in.1, s32[64,128]{1,0:T(8,128)} %bitcast.8), custom_call_target="tpu_custom_call" | custom-call | tf_op jit(solution)/shard_map/pallas_call | solution.py:516
  61.2 3.9 %shard_map.87 = (f32[7,4,16,128]{3,2,1,0:T(8,128)}, f32[3,8192]{1,0:T(4,128)}) custom-call(f32[8,16,2,128]{3,2,1,0:T(2,128)} %get-tuple-element.4.landed, s32[64,128]{1,0:T(8,128)} %bitcast.9, f32[7,4,16,128]{3,2,1,0:T(8,128)} %get-tuple-element.5.computed), custom_call_target="tpu_custom_call" | custom-call | tf_op jit(solution)/shard_map/pallas_call | solution.py:552
